TPU v7x, 32 devices: a whole 2x2x4 slice. The times are simulated.
32 devices in a mesh: dp: 4 (over x, core), ctx: 8 (over z, y).
Axes of the slice: x: 2, y: 2, z: 4, core: 2. Of those that a mesh axis runs over, the one named last changes fastest.
Arguments:
- inputs: bfloat16 [32, 1024, 768], P('dp', 'ctx'), may hold values from -6 to 6
- segments: int32 [32, 1024], P('dp'), may hold values from 0 to 5, as said below
- random_blocks: int32 [32, 16, 12, 3], P('dp', 'ctx'), may hold values from 0 to 15, as said below
- cotangent: bfloat16 [32, 1024, 768], P('dp', 'ctx'), may hold values from -6 to 6
- qkv_weight: bfloat16 [768, 2304], P('dp'), may hold values from -0.21875 to 0.21875
- qv_bias: bfloat16 [1536], P('dp'), may hold values from -2 to 2
- out_weight: bfloat16 [768, 768], P('dp'), may hold values from -3.5 to 3.5
- out_bias: bfloat16 [768], P('dp'), may hold values from -2 to 2
- norm1_gain: bfloat16 [768], P('dp'), may hold values from 0.5 to 1.5
- norm1_bias: bfloat16 [768], P('dp'), may hold values from -2 to 2
- up_weight: bfloat16 [768, 3072], P('dp'), may hold values from -0.21875 to 0.21875
- up_bias: bfloat16 [3072], P('dp'), may hold values from -2 to 2
- down_weight: bfloat16 [3072, 768], P('dp'), may hold values from -0.109375 to 0.109375
- down_bias: bfloat16 [768], P('dp'), may hold values from -2 to 2
- norm2_gain: bfloat16 [768], P('dp'), may hold values from 0.5 to 1.5
- norm2_bias: bfloat16 [768], P('dp'), may hold values from -2 to 2
Outputs:
- layer_out: bfloat16 [32, 1024, 768], P('dp', 'ctx')
- input_grad: bfloat16 [32, 1024, 768], P('dp', 'ctx')
- grad_qkv_weight: float32 [768, 2304], P('dp')
- grad_qv_bias: float32 [1536], P('dp')
- grad_out_weight: float32 [768, 768], P('dp')
- grad_out_bias: float32 [768], P('dp')
- grad_norm1_gain: float32 [768], P('dp')
- grad_norm1_bias: float32 [768], P('dp')
- grad_up_weight: float32 [768, 3072], P('dp')
- grad_up_bias: float32 [3072], P('dp')
- grad_down_weight: float32 [3072, 768], P('dp')
- grad_down_bias: float32 [768], P('dp')
- grad_norm2_gain: float32 [768], P('dp')
- grad_norm2_bias: float32 [768], P('dp')
Inputs may be any that keep to these rules, and one draw needn't show every extreme that they name: `segments`: segment numbers start at 0 and never fall along a sequence. In each group of 8 sequences that share an index of dp, one sequence is a single document and another packs documents of exactly 200 tokens; the others pack documents of 200 to 2000 tokens; in every packed sequence the last document is cut by the sequence's end. `random_blocks`: for each group of 8 sequences that share an index of dp and each aligned run of 2 query blocks, the entries over those sequences, blocks, heads and slots name blocks of every aligned run of 2 key blocks exactly 72 times.
All inputs are finite; a program needn't handle non-finite values.
Results may differ from a plain program's by a relative error of at most 0.015.
Values may be sent and summed in bfloat16 or wider, within the bound.
No kernel may reach another device: no remote copies, remote signals or barrier semaphores. Data moves between devices by JAX's collectives and lax.ppermute only.
A program may use at most 576 MiB of HBM per device.

v0:
```python
import functools

import jax
import jax.numpy as jnp
from jax import lax
from jax.experimental import pallas as pl
from jax.experimental.pallas import tpu as pltpu
from jax.sharding import PartitionSpec as P

f32, bf16 = jnp.float32, jnp.bfloat16
eps_norm = 1e-12
far = 1e30
doc_min = 200
lanes_n = 128
vmem_cap = 56 * 2**20


def swap_pieces(pieces, axis, stride):
    count, size = pieces.shape[0], lax.axis_size(axis)
    groups = None
    if count < size:
        span = stride * count
        starts = [base + offset for base in range(0, size, span) for offset in range(stride)]
        groups = [[start + i * stride for i in range(count)] for start in starts]
    return lax.all_to_all(pieces, axis, 0, 0, axis_index_groups=groups, tiled=True)


def share_pieces(piece, axis, count):
    size = lax.axis_size(axis)
    member = lax.axis_index(axis) % count
    came, stride = piece[None], 1
    while stride < count:
        other = lax.ppermute(came, axis, [(i, i ^ stride) for i in range(size)])
        upper = (member // stride) % 2 == 1
        came = jnp.concatenate([jnp.where(upper, other, came), jnp.where(upper, came, other)], axis=0)
        stride *= 2
    return came


def tied(value, *deps):
    def nothing(*refs):
        pass

    return pl.pallas_call(
        nothing,
        in_specs=[pl.BlockSpec(memory_space=pl.ANY)] * (1 + len(deps)),
        out_specs=pl.BlockSpec(memory_space=pl.ANY),
        out_shape=jax.ShapeDtypeStruct(value.shape, value.dtype),
        input_output_aliases={0: 0},
        name="tied",
    )(value, *deps)


def added(terms):
    if len(terms) == 1:
        return terms[0]
    total = terms[0].astype(f32)
    for term in terms[1:]:
        total = total + term.astype(f32)
    return total.astype(bf16)


class Chain:
    def __init__(self, parts, axis="ctx"):
        self.parts = parts
        strides, stride = [], 1
        while stride < lax.axis_size(axis):
            strides.append(stride)
            stride *= 2
        self.axis = axis
        self.plan = [(stride, True) for stride in strides]
        if axis == "ctx":
            self.plan += [(stride, False) for stride in reversed(strides)]

    def halves(self, stride):
        member = (lax.axis_index(self.axis) // stride) % 2

        def half(which):
            columns = []
            for terms in self.parts:
                rows = terms[0].shape[0] // 2
                cut = [lax.dynamic_slice_in_dim(term, which * rows, rows, 0) for term in terms]
                columns.append(added(cut))
            return columns[0] if len(columns) == 1 else jnp.concatenate(columns, axis=1)

        return half(member), half(1 - member)

    def begin(self, *after):
        stride, adds = self.plan[0]
        if adds:
            self.kept, sent = self.halves(stride)
            sent = tied(sent, *after)
        else:
            sent = tied(added(self.parts[0]), *after)
            self.kept = sent
        size = lax.axis_size(self.axis)
        self.came = lax.ppermute(sent, self.axis, [(i, i ^ stride) for i in range(size)])
        return sent

    def end(self, *after):
        stride, adds = self.plan.pop(0)
        came = tied(self.came, *after) if after else self.came
        if adds:
            self.parts = [[self.kept, came]]
        else:
            upper = (lax.axis_index(self.axis) // stride) % 2 == 1
            pair = [jnp.where(upper, came, self.kept), jnp.where(upper, self.kept, came)]
            self.parts = [[jnp.concatenate(pair, axis=0)]]
        return self.parts[0]

    def next(self, *after):
        self.end()
        return self.begin(*after)

    def open(self):
        return len(self.plan) > 0


class Scatter:
    def __init__(self, kept, sent):
        self.kept, self.came, self.stride = kept, None, 1
        self.sent = sent

    def begin(self, *after):
        size = lax.axis_size("dp")
        sent = tied(self.sent, *after)
        self.came = lax.ppermute(sent, "dp", [(i, i ^ self.stride) for i in range(size)])
        return sent

    def end(self, *after):
        came = tied(self.came, *after) if after else self.came
        self.stride *= 2
        if self.stride == lax.axis_size("dp"):
            return [self.kept, came]
        rows = self.kept.shape[0] // 2
        self.sent = added([self.kept[rows:], came[rows:]])
        self.kept = added([self.kept[:rows], came[:rows]])
        return None


def copied(value, *deps):
    def copy(value_ref, *refs):
        refs[-1][...] = value_ref[...]

    return pl.pallas_call(
        copy,
        in_specs=[pl.BlockSpec(memory_space=pltpu.VMEM)]
        + [pl.BlockSpec(memory_space=pl.ANY)] * len(deps),
        out_shape=jax.ShapeDtypeStruct(value.shape, value.dtype),
        name="copied",
    )(value, *deps)


def scattered(grad):
    return lax.psum_scatter(grad, "dp", scatter_dimension=0, tiled=True)


def mask_features(seg, rand, block):
    tokens = seg.shape[0]
    blocks, heads = rand.shape[:2]
    seg_limit = tokens // doc_min + 1
    used = seg_limit + 2 * blocks
    width = -(-used // lanes_n) * lanes_n
    ids = jnp.arange(blocks, dtype=jnp.int32)

    def hot(values):
        return (values[..., None] == ids).astype(jnp.int32)

    near = hot(ids - 1) + hot(ids) + hot(ids + 1) + hot(ids * 0) + hot(ids * 0 + blocks - 1)
    counts = near[:, None, :] + jnp.sum(hot(rand), axis=2)
    edge = (ids == 0) | (ids == blocks - 1)
    counts = jnp.where(edge[:, None, None], 1, counts).transpose(1, 2, 0)
    log_count = jnp.log(jnp.maximum(counts, 1).astype(f32))
    high = log_count.astype(bf16).astype(f32)
    low = jnp.where(counts > 0, log_count - high, 0.0)
    high = jnp.where(counts > 0, high, -far)
    table = jnp.concatenate(
        [
            jnp.zeros((heads, blocks, seg_limit), f32),
            high,
            low,
            jnp.zeros((heads, blocks, width - used), f32),
        ],
        axis=2,
    )
    lane = jnp.arange(width, dtype=jnp.int32)[None]
    own = (jnp.arange(tokens, dtype=jnp.int32) // block)[:, None]
    is_seg = lane < seg_limit
    same = lane == seg[:, None]
    key_feat = jnp.where(is_seg & same, 1.0, 0.0).astype(bf16)
    own_lane = (lane - seg_limit == own) | (lane - seg_limit - blocks == own)
    query_feat = jnp.where(
        is_seg, jnp.where(same, 0.0, -far), jnp.where(own_lane, 1.0, 0.0)
    ).astype(bf16)
    near = -(-seg_limit // lanes_n) * lanes_n
    return key_feat[:, :near], query_feat[:, :near], table


def fill_keys(k_ref, key_feat_ref, table_ref, keys):
    tokens, near = key_feat_ref.shape
    blocks, width = table_ref.shape[1:]
    feat = key_feat_ref[...].astype(f32).reshape(blocks, tokens // blocks, near)
    for side in range(2):
        rows = table_ref[side][:, None, :]
        both = (feat + rows[..., :near]).reshape(tokens, near)
        keys[side, :, :lanes_n] = k_ref[...]
        keys[side, :, lanes_n : lanes_n + near] = both.astype(bf16)
        if width > near:
            rest = jnp.broadcast_to(rows[..., near:], (blocks, tokens // blocks, width - near))
            keys[side, :, lanes_n + near :] = rest.reshape(tokens, width - near).astype(bf16)


def query_lanes(near_feat, start, tokens, blocks, width):
    rows, near = near_feat.shape
    if width == near:
        return near_feat
    shape = (rows, width - near)
    lane = lax.broadcasted_iota(jnp.int32, shape, 1) + near - (tokens // doc_min + 1)
    own = (lax.broadcasted_iota(jnp.int32, shape, 0) + start) // (tokens // blocks)
    rest = jnp.where((lane == own) | (lane - blocks == own), 1.0, 0.0).astype(bf16)
    return jnp.concatenate([near_feat, rest], axis=1)


rows_by_rows = (((1,), (1,)), ((), ()))
cols_by_cols = (((0,), (0,)), ((), ()))


def dot(left, right, dims=(((1,), (0,)), ((), ()))):
    return lax.dot_general(left, right, dims, preferred_element_type=f32)


def forward_kernel(
    q_ref, k_ref, v_ref, key_feat_ref, query_feat_ref, table_ref, out_ref, keys, vals, *, half, tile
):
    tokens = q_ref.shape[0]
    fill_keys(k_ref, key_feat_ref, table_ref, keys)
    vals[:, :lanes_n] = v_ref[...]
    vals[:, lanes_n:] = jnp.ones((tokens, lanes_n), bf16)

    @pl.loop(0, tokens // tile)
    def _(step):
        rows = pl.ds(pl.multiple_of(step * tile, tile), tile)
        q = q_ref[rows, :] * bf16(half**-0.5)
        side_of = lax.broadcasted_iota(jnp.int32, (tile, lanes_n), 1) // half
        feat = query_lanes(query_feat_ref[rows, :], step * tile, tokens, *table_ref.shape[1:])
        scores = [
            dot(
                jnp.concatenate([jnp.where(side_of == side, q, bf16(0)), feat], axis=1),
                keys[side],
                rows_by_rows,
            )
            for side in range(2)
        ]
        outs = []
        for score in scores:
            weights = jnp.exp(score - jnp.max(score, axis=1, keepdims=True)).astype(bf16)
            mixed = dot(weights, vals[...])
            outs.append(mixed[:, :lanes_n] / mixed[:, lanes_n:])
        out_ref[rows, :] = jnp.where(side_of == 0, outs[0], outs[1]).astype(bf16)


def backward_kernel(
    q_ref,
    k_ref,
    v_ref,
    grad_ref,
    key_feat_ref,
    query_feat_ref,
    table_ref,
    dq_ref,
    dk_ref,
    dv_ref,
    sums_ref,
    keys,
    dk_sum,
    dv_sum,
    *,
    half,
    tile,
):
    tokens = q_ref.shape[0]
    fill_keys(k_ref, key_feat_ref, table_ref, keys)
    dk_sum[...] = jnp.zeros_like(dk_sum)
    dv_sum[...] = jnp.zeros_like(dv_sum)
    sums_ref[...] = jnp.zeros_like(sums_ref)

    @pl.loop(0, tokens // tile)
    def _(step):
        rows = pl.ds(pl.multiple_of(step * tile, tile), tile)
        q_pair = q_ref[rows, :] * bf16(half**-0.5)
        grad_pair = grad_ref[rows, :]
        side_of = lax.broadcasted_iota(jnp.int32, (tile, lanes_n), 1) // half
        feat = query_lanes(query_feat_ref[rows, :], step * tile, tokens, *table_ref.shape[1:])
        queries = [jnp.where(side_of == side, q_pair, bf16(0)) for side in range(2)]
        grads = [jnp.where(side_of == side, grad_pair, bf16(0)) for side in range(2)]
        probs, dscores = [], []
        for side in range(2):
            wide = jnp.concatenate([queries[side], feat], axis=1)
            scores = dot(wide, keys[side], rows_by_rows)
            dprobs = dot(grads[side], v_ref[...], rows_by_rows)
            raw = jnp.exp(scores - jnp.max(scores, axis=1, keepdims=True))
            prob = raw * (1.0 / jnp.sum(raw, axis=1, keepdims=True))
            both = prob * dprobs
            dscore = both - prob * jnp.sum(both, axis=1, keepdims=True)
            probs.append(prob.astype(bf16))
            dscores.append(dscore.astype(bf16))
        dv_sum[...] += dot(
            jnp.concatenate(probs, axis=0), jnp.concatenate(grads, axis=0), cols_by_cols
        )
        dk_sum[...] += dot(
            jnp.concatenate(dscores, axis=0), jnp.concatenate(queries, axis=0), cols_by_cols
        )
        dqs = [dot(dscore, k_ref[...]) for dscore in dscores]
        dq = (jnp.where(side_of == 0, dqs[0], dqs[1]) * half**-0.5).astype(bf16)
        dq_ref[rows, :] = dq
        sums_ref[0:1, :] += jnp.sum(dq.astype(f32), axis=0, keepdims=True)

    dk_ref[...] = dk_sum[...].astype(bf16)
    dv = dv_sum[...].astype(bf16)
    dv_ref[...] = dv
    sums_ref[1:2, :] = jnp.sum(dv.astype(f32), axis=0, keepdims=True)


def attend(kernel, arrays, features, outs, half, name, after=(), first=0, count=None):
    tokens, width = arrays[0].shape
    key_feat, query_feat, table = features
    count = width // lanes_n if count is None else count
    near, feat_width = key_feat.shape[1], table.shape[2]
    tile = tokens if tokens <= 1024 else 32
    once = {"pipeline_mode": pl.Buffered(1)} if count == 1 else {}
    pair = pl.BlockSpec((tokens, lanes_n), lambda p: (0, p + first), **once)
    pair_out = pl.BlockSpec((tokens, lanes_n), lambda p: (0, p), **once)
    whole = pl.BlockSpec((tokens, near), lambda p: (0, 0), pipeline_mode=pl.Buffered(1))
    shape = jax.ShapeDtypeStruct((tokens, count * lanes_n), bf16)
    scratch = [pltpu.VMEM((2, tokens, lanes_n + feat_width), bf16)]
    if outs == 1:
        scratch = scratch + [pltpu.VMEM((tokens, 2 * lanes_n), bf16)]
    else:
        scratch = scratch + [pltpu.VMEM((tokens, lanes_n), f32)] * 2

    def run(*refs):
        held = len(arrays) + 3
        kernel(*refs[:held], *refs[held + len(after) :], half=half, tile=tile)

    return pl.pallas_call(
        run,
        grid=(count,),
        in_specs=[pair] * len(arrays)
        + [whole, whole]
        + [pl.BlockSpec((2,) + table.shape[1:], lambda p: (p + first, 0, 0))]
        + [pl.BlockSpec(memory_space=pl.ANY)] * len(after),
        out_specs=[pair_out] * outs + [pl.BlockSpec((8, lanes_n), lambda p: (0, p))] * (outs > 1),
        out_shape=[shape] * outs
        + [jax.ShapeDtypeStruct((8, count * lanes_n), f32)] * (outs > 1),
        scratch_shapes=scratch,
        compiler_params=pltpu.CompilerParams(vmem_limit_bytes=vmem_cap),
        cost_estimate=pl.CostEstimate(flops=0, bytes_accessed=tokens, transcendentals=0),
        name=name,
    )(*arrays, key_feat, query_feat, table, *after)


def pack_kernel(weight_ref, *refs):
    out_ref = refs[-1]
    rows = weight_ref.shape[0]
    out_ref[:rows, :] = weight_ref[...]
    out_ref[rows:, :] = jnp.zeros_like(out_ref[rows:, :])
    for place, ref in enumerate(refs[:-1]):
        out_ref[rows + place : rows + place + 1, : ref.shape[0]] = ref[...].reshape(1, -1)


def pack_weights(weight, vectors):
    rows, cols = weight.shape
    extra = -(-len(vectors) // 16) * 16
    return pl.pallas_call(
        pack_kernel,
        out_shape=jax.ShapeDtypeStruct((rows + extra, cols), weight.dtype),
        name="pack_weights",
    )(weight, *vectors)


def join_kernel(out_ref, up_ref, down_ref, all_ref):
    rows, width = out_ref.shape
    hidden_n = up_ref.shape[1]
    all_ref[:, :width] = out_ref[...]
    all_ref[:, width : width + hidden_n] = up_ref[...]
    for part in range(hidden_n // width):
        start = width + hidden_n + part * width
        all_ref[:, start : start + width] = down_ref[part * rows : (part + 1) * rows, :]


def join_weights(out_weight, up_weight, down_weight):
    rows, width = out_weight.shape
    return pl.pallas_call(
        join_kernel,
        out_shape=jax.ShapeDtypeStruct((rows, width + 2 * up_weight.shape[1]), out_weight.dtype),
        compiler_params=pltpu.CompilerParams(vmem_limit_bytes=vmem_cap),
        name="join_weights",
    )(out_weight, up_weight, down_weight)


def project_kernel(x_ref, weight_ref, bias_ref, q_ref, k_ref, v_ref, weight, *, part):
    shards = weight_ref.shape[0]
    width = x_ref.shape[1]

    @pl.when(pl.program_id(0) == 0)
    def _():
        for shard in range(shards):
            weight[shard * part : (shard + 1) * part, :] = weight_ref[shard, :part, :]

    x = x_ref[...]
    q_ref[...] = (dot(x, weight[:, :width]) + bias_ref[:, :width]).astype(bf16)
    k_ref[...] = dot(x, weight[:, width : 2 * width]).astype(bf16)
    v_ref[...] = (dot(x, weight[:, 2 * width :]) + bias_ref[:, width:]).astype(bf16)


def project(x, weight, bias):
    tokens, width = x.shape
    tile = min(512, tokens)
    row = pl.BlockSpec((tile, width), lambda i: (i, 0))
    shape = jax.ShapeDtypeStruct((tokens, width), bf16)
    return pl.pallas_call(
        functools.partial(project_kernel, part=width // weight.shape[0]),
        grid=(tokens // tile,),
        in_specs=[
            row,
            pl.BlockSpec(weight.shape, lambda i: (0, 0, 0), pipeline_mode=pl.Buffered(1)),
            pl.BlockSpec(bias.shape, lambda i: (0, 0)),
        ],
        out_specs=[row] * 3,
        out_shape=[shape] * 3,
        scratch_shapes=[pltpu.VMEM((width, weight.shape[2]), bf16)],
        compiler_params=pltpu.CompilerParams(vmem_limit_bytes=vmem_cap),
        cost_estimate=pl.CostEstimate(flops=0, bytes_accessed=tokens, transcendentals=0),
        name="project",
    )(x, weight, bias)


def sort_shards(place_ref, grad, kept_ref, sent_ref, shards, block, block_n):
    rows = grad.shape[0] // shards
    for shard in range(shards):
        turn = place_ref[0] ^ shard
        start = pl.multiple_of(((turn // 2) * block_n + block) * rows, rows)
        piece = grad[shard * rows : (shard + 1) * rows].astype(bf16)

        @pl.when(turn % 2 == 0)
        def _():
            kept_ref[pl.ds(start, rows), : grad.shape[1]] = piece

        @pl.when(turn % 2 == 1)
        def _():
            sent_ref[pl.ds(start, rows), : grad.shape[1]] = piece


def grads_kernel(place_ref, *refs, groups, held, shards):
    kept_ref, sent_ref = refs[-2:]
    grads = []
    for left, rights in groups:
        right = [refs[place][...] for place in rights]
        right = right[0] if len(right) == 1 else jnp.concatenate(right, axis=1)
        grads.append(dot(refs[left][...], right, cols_by_cols).astype(bf16))
    grads.append(jnp.transpose(refs[held - 1][...]).astype(bf16))
    sort_shards(place_ref, jnp.concatenate(grads, axis=1), kept_ref, sent_ref, shards, 0, 1)


def weight_grads(place, groups, extra, shards, after=()):
    arrays, places = [], []
    for left, rights in groups:
        places.append((len(arrays), tuple(range(len(arrays) + 1, len(arrays) + 1 + len(rights)))))
        arrays += [left] + list(rights)
    arrays.append(extra)
    cols = sum(right.shape[1] for _, rights in groups for right in rights) + extra.shape[0]
    held = len(arrays)
    half = jax.ShapeDtypeStruct((groups[0][0].shape[1] // 2, cols), bf16)
    return pl.pallas_call(
        functools.partial(grads_kernel, groups=places, held=held, shards=shards),
        in_specs=[pl.BlockSpec(memory_space=pltpu.SMEM)]
        + [pl.BlockSpec(memory_space=pltpu.VMEM)] * held
        + [pl.BlockSpec(memory_space=pl.ANY)] * len(after),
        out_shape=[half] * 2,
        compiler_params=pltpu.CompilerParams(vmem_limit_bytes=vmem_cap),
        cost_estimate=pl.CostEstimate(flops=0, bytes_accessed=cols, transcendentals=0),
        name="weight_grads",
    )(place, *arrays, *after)


def wide_grad_kernel(place_ref, left_ref, right_ref, *refs, shards):
    grad = dot(left_ref[...], right_ref[...], cols_by_cols)
    sort_shards(
        place_ref, grad, refs[-2], refs[-1], shards, pl.program_id(0), pl.num_programs(0)
    )


def wide_grad(place, left, right, shards, after=()):
    tokens, rows = left.shape
    runs = right.shape[1] // rows
    half = (rows * runs // 2, rows)
    whole = pl.BlockSpec(half, lambda i: (0, 0))
    return pl.pallas_call(
        functools.partial(wide_grad_kernel, shards=shards),
        grid=(runs,),
        in_specs=[
            pl.BlockSpec(memory_space=pltpu.SMEM),
            pl.BlockSpec((tokens, rows), lambda i: (0, 0)),
            pl.BlockSpec((tokens, rows), lambda i: (0, i)),
        ]
        + [pl.BlockSpec(memory_space=pl.ANY)] * len(after),
        out_specs=[whole] * 2,
        out_shape=[jax.ShapeDtypeStruct(half, bf16)] * 2,
        compiler_params=pltpu.CompilerParams(vmem_limit_bytes=vmem_cap),
        cost_estimate=pl.CostEstimate(flops=0, bytes_accessed=rows, transcendentals=0),
        name="wide_grad",
    )(place, left, right, *after)


def matrix_grad_kernel(left_ref, right_ref, *refs):
    refs[-1][...] = dot(left_ref[...], right_ref[...], cols_by_cols).astype(bf16)


def matrix_grad(left, right, after=()):
    tokens, rows = left.shape
    cols = right.shape[1]
    run = min(rows, cols)
    tall = rows > cols

    def taken(yes):
        return pl.BlockSpec((tokens, run), (lambda i: (0, i)) if yes else (lambda i: (0, 0)))

    return pl.pallas_call(
        matrix_grad_kernel,
        grid=(max(rows, cols) // run,),
        in_specs=[taken(tall), taken(not tall)] + [pl.BlockSpec(memory_space=pl.ANY)] * len(after),
        out_specs=pl.BlockSpec((run, run), (lambda i: (i, 0)) if tall else (lambda i: (0, i))),
        out_shape=jax.ShapeDtypeStruct((rows, cols), bf16),
        compiler_params=pltpu.CompilerParams(vmem_limit_bytes=vmem_cap),
        cost_estimate=pl.CostEstimate(flops=0, bytes_accessed=cols, transcendentals=0),
        name="matrix_grad",
    )(left, right, *after)


def input_kernel(*refs, part, parts_n):
    weight_ref, pre_ref = refs[0], refs[1]
    out_ref, weight = refs[-2], refs[-1]
    shards = weight_ref.shape[0]

    @pl.when(pl.program_id(0) == 0)
    def _():
        for shard in range(shards):
            weight[shard * part : (shard + 1) * part, :] = weight_ref[shard, :part, :]

    grads = jnp.concatenate([ref[...] for ref in refs[2 : 2 + parts_n]], axis=1)
    out_ref[...] = (pre_ref[...] + dot(grads, weight[...], rows_by_rows)).astype(bf16)


def input_gradient(weight, grad_pre, parts, after):
    tokens, width = grad_pre.shape
    tile = min(512, tokens)

    def row(n):
        return pl.BlockSpec((tile, n), lambda i: (i, 0))

    return pl.pallas_call(
        functools.partial(input_kernel, part=width // weight.shape[0], parts_n=len(parts)),
        grid=(tokens // tile,),
        in_specs=[pl.BlockSpec(weight.shape, lambda i: (0, 0, 0), pipeline_mode=pl.Buffered(1))]
        + [row(width)]
        + [row(part.shape[1]) for part in parts]
        + [pl.BlockSpec(memory_space=pl.ANY)] * len(after),
        out_specs=row(width),
        out_shape=jax.ShapeDtypeStruct((tokens, width), bf16),
        scratch_shapes=[pltpu.VMEM((width, weight.shape[2]), bf16)],
        compiler_params=pltpu.CompilerParams(vmem_limit_bytes=vmem_cap),
        cost_estimate=pl.CostEstimate(flops=0, bytes_accessed=tokens, transcendentals=0),
        name="input_gradient",
    )(weight, grad_pre, *parts, *after)


def token_kernel(
    attended_ref,
    x_ref,
    cot_ref,
    weights_ref,
    vec_ref,
    bias_up_ref,
    out_ref,
    hidden_ref,
    active_ref,
    grad_mlp_ref,
    grad_upper_ref,
    grad_pre_ref,
    grad_branch_ref,
    grad_attended_ref,
    sums_ref,
    sums_up_ref,
    weight_out,
    weight_up,
    weight_down,
    slope,
    arrived,
):
    shards, part = weights_ref.shape[:2]
    width, hidden_n = weight_up.shape
    chunks = hidden_n // width

    copies = [[], [], []]
    for shard in range(shards):
        rows = pl.ds(shard * part, part)
        mine = weights_ref.at[shard]
        copies[0].append((mine.at[:, pl.ds(0, width)], weight_out.at[rows, :]))
        copies[1].append((mine.at[:, pl.ds(width, hidden_n)], weight_up.at[rows, :]))
        for chunk in range(chunks):
            start = width + hidden_n + chunk * width
            rows = pl.ds((shard * chunks + chunk) * part, part)
            copies[2].append((mine.at[:, pl.ds(start, width)], weight_down.at[rows, :]))
    starts = [0, shards, 2 * shards]
    copies = [
        [
            pltpu.make_async_copy(source, target, arrived.at[start + place])
            for place, (source, target) in enumerate(some)
        ]
        for start, some in zip(starts, copies)
    ]

    def wait_for(place):
        @pl.when(pl.program_id(0) == 0)
        def _():
            for copy in copies[place]:
                copy.wait()

    @pl.when(pl.program_id(0) == 0)
    def _():
        for some in copies:
            for copy in some:
                copy.start()
        sums_ref[...] = jnp.zeros_like(sums_ref)
        sums_up_ref[...] = jnp.zeros_like(sums_up_ref)

    bias_out, gain_one, shift_one, bias_down, gain_two, shift_two = [
        vec_ref[place : place + 1, :] for place in range(6)
    ]

    def mean(value):
        return jnp.mean(value, axis=1, keepdims=True)

    def add_to(place, value):
        sums_ref[place : place + 1, :] += jnp.sum(value.astype(f32), axis=0, keepdims=True)

    def normed(value):
        centred = value - mean(value)
        inverse = lax.rsqrt(mean(centred * centred) + eps_norm)
        return centred * inverse, inverse

    def norm_backward(incoming, normed_value, inverse, gain):
        scaled = incoming * gain
        centred = scaled - mean(scaled) - normed_value * mean(scaled * normed_value)
        return centred * inverse

    wait_for(0)
    branch = dot(attended_ref[...], weight_out[...]) + bias_out
    normed_one, inverse_one = normed(x_ref[...].astype(f32) + branch)
    hidden = normed_one * gain_one + shift_one
    hidden_low = hidden.astype(bf16)
    hidden_ref[...] = hidden_low
    mlp_out = jnp.zeros_like(hidden)
    wait_for(1)
    wait_for(2)
    for chunk in range(chunks):
        cols = slice(chunk * width, (chunk + 1) * width)
        upper = dot(hidden_low, weight_up[:, cols]) + bias_up_ref[:, cols]
        share = 0.5 * (1.0 + lax.erf(upper * 0.5**0.5))
        density = jnp.exp(-0.5 * upper * upper) * (2.0 * jnp.pi) ** -0.5
        active = (upper * share).astype(bf16)
        active_ref[:, cols] = active
        slope[:, cols] = share + upper * density
        mlp_out = mlp_out + dot(active, weight_down[cols, :])
    normed_two, inverse_two = normed(hidden + (mlp_out + bias_down))
    out_ref[...] = (normed_two * gain_two + shift_two).astype(bf16)

    incoming = cot_ref[...].astype(f32)
    grad_sum = norm_backward(incoming, normed_two, inverse_two, gain_two)
    grad_mlp = grad_sum.astype(bf16)
    grad_mlp_ref[...] = grad_mlp
    add_to(5, incoming)
    add_to(4, incoming * normed_two)
    add_to(3, grad_mlp)
    grad_hidden = grad_sum
    for chunk in range(chunks):
        cols = slice(chunk * width, (chunk + 1) * width)
        grad_active = dot(grad_mlp, weight_down[cols, :], rows_by_rows)
        grad_upper = (grad_active * slope[:, cols]).astype(bf16)
        grad_upper_ref[:, cols] = grad_upper
        sums_up_ref[0:1, cols] += jnp.sum(grad_upper.astype(f32), axis=0, keepdims=True)
        grad_hidden = grad_hidden + dot(grad_upper, weight_up[:, cols], rows_by_rows)
    grad_pre = norm_backward(grad_hidden, normed_one, inverse_one, gain_one)
    grad_pre_ref[...] = grad_pre
    grad_branch = grad_pre.astype(bf16)
    grad_branch_ref[...] = grad_branch
    add_to(2, grad_hidden)
    add_to(1, grad_hidden * normed_one)
    add_to(0, grad_branch)
    grad_attended_ref[...] = dot(grad_branch, weight_out[...], rows_by_rows).astype(bf16)


def token_parts(attended, x, cotangent, weights, vecs, bias_up):
    tokens, width = x.shape
    shards, part, cols = weights.shape
    hidden_n = (cols - width) // 2
    tile = 256

    def row(n):
        return pl.BlockSpec((tile, n), lambda i: (i, 0))

    def fixed(shape):
        return pl.BlockSpec(shape, lambda i: (0, 0))

    def shape(n, kind=bf16):
        return jax.ShapeDtypeStruct((tokens, n), kind)

    copies = shards * (2 + hidden_n // width)
    return pl.pallas_call(
        token_kernel,
        grid=(tokens // tile,),
        in_specs=[row(width)] * 3
        + [pl.BlockSpec(memory_space=pl.ANY), fixed(vecs.shape), fixed(bias_up.shape)],
        out_specs=[
            row(width),
            row(width),
            row(hidden_n),
            row(width),
            row(hidden_n),
            row(width),
            row(width),
            row(width),
            fixed((8, width)),
            fixed((8, hidden_n)),
        ],
        out_shape=[
            shape(width),
            shape(width),
            shape(hidden_n),
            shape(width),
            shape(hidden_n),
            shape(width, f32),
            shape(width),
            shape(width),
            jax.ShapeDtypeStruct((8, width), f32),
            jax.ShapeDtypeStruct((8, hidden_n), f32),
        ],
        scratch_shapes=[
            pltpu.VMEM((width, width), bf16),
            pltpu.VMEM((width, hidden_n), bf16),
            pltpu.VMEM((hidden_n, width), bf16),
            pltpu.VMEM((tile, hidden_n), f32),
            pltpu.SemaphoreType.DMA((copies,)),
        ],
        compiler_params=pltpu.CompilerParams(vmem_limit_bytes=vmem_cap),
        cost_estimate=pl.CostEstimate(flops=0, bytes_accessed=tokens, transcendentals=0),
        name="token_parts",
    )(attended, x, cotangent, weights, vecs, bias_up)


def body(
    inputs,
    segments,
    random_blocks,
    cotangent,
    qkv_weight,
    qv_bias,
    out_weight,
    out_bias,
    norm1_gain,
    norm1_bias,
    up_weight,
    up_bias,
    down_weight,
    down_bias,
    norm2_gain,
    norm2_bias,
):
    seq_count, run, width = inputs.shape
    per_dev, head_count, rand_count = random_blocks.shape[1:]
    block = run // per_dev
    head_size = width // head_count
    dp_count = lax.axis_size("dp")
    ctx_count = lax.axis_size("ctx")
    ctx_index = lax.axis_index("ctx")
    team = ctx_count // seq_count
    tokens = seq_count * run

    x = swap_pieces(inputs, "ctx", team).reshape(tokens, width)
    lists = swap_pieces(tied(random_blocks.reshape(seq_count, 1, -1), x), "ctx", team)

    def back_to_runs(rows):
        return swap_pieces(rows.reshape(seq_count, run, width), "ctx", team)

    vectors = (qv_bias, out_bias, norm1_gain, norm1_bias, up_bias, down_bias, norm2_gain, norm2_bias)
    sizes = [v.shape[0] for v in vectors]
    qkv_rows, qkv_cols = qkv_weight.shape
    first = lax.all_gather(pack_weights(qkv_weight, vectors), "dp", axis=0)
    others = lax.all_gather(join_weights(out_weight, up_weight, down_weight), "dp", axis=0)

    def vector(place):
        return first[:, qkv_rows + place, : sizes[place]].reshape(1, -1).astype(f32)

    bias_qv, bias_up = vector(0), vector(4)
    vecs = first[:, qkv_rows + 1 : qkv_rows + 8, :qkv_rows].transpose(1, 0, 2).reshape(7, width)
    vecs = jnp.concatenate([vecs[:3], vecs[4:], jnp.zeros_like(vecs[:2])], axis=0).astype(f32)

    seq_index = ctx_index // team
    seg = lax.dynamic_index_in_dim(segments, seq_index, 0, keepdims=False)
    lists = lists.reshape(seq_count, per_dev, head_count, rand_count)
    if team > 1:
        team_index = ctx_index % team
        held = -(-head_count // (2 * team)) * 2
        spare = held * team - head_count
        lists = share_pieces(lists, "ctx", team).transpose(1, 0, 2, 3, 4)
        lists = jnp.pad(lists.reshape(-1, head_count, rand_count), ((0, 0), (0, spare), (0, 0)))
        lists = lax.dynamic_slice_in_dim(lists, team_index * held, held, 1)
    else:
        lists = lists.reshape(-1, head_count, rand_count)
    features = mask_features(seg, lists, block)

    def to_heads(rows):
        if team == 1:
            return rows
        rows = jnp.pad(rows, ((0, 0), (0, spare * head_size)))
        part = swap_pieces(rows.reshape(tokens, team, -1).transpose(1, 0, 2), "ctx", 1)
        part = part.reshape(team, seq_count, run, -1).transpose(1, 0, 2, 3)
        return part.reshape(team * tokens, -1)

    def to_tokens(part):
        if team == 1:
            return part
        part = part.reshape(seq_count, team, run, -1).transpose(1, 0, 2, 3)
        rows = swap_pieces(part.reshape(team, tokens, -1), "ctx", 1)
        return rows.transpose(1, 0, 2).reshape(tokens, -1)[:, :width]

    queries, keys, values = project(x, first, bias_qv)
    grad_result = swap_pieces(copied(cotangent, x), "ctx", team).reshape(tokens, width)
    heads = tuple(to_heads(part) for part in (queries, keys, values))
    attended = attend(forward_kernel, heads, features, 1, head_size, "attend_forward")[0]
    attended = to_tokens(attended)
    parts = token_parts(attended, x, grad_result, others, vecs, bias_up)
    result, hidden_low, active, grad_mlp, grad_upper, grad_pre, grad_branch, grad_att, sums, sums_up = parts

    down_grad = matrix_grad(active, grad_mlp)
    down_part = scattered(down_grad)
    place = lax.axis_index("dp").reshape(1).astype(jnp.int32)
    up = Scatter(*wide_grad(place, hidden_low, grad_upper, dp_count, (down_grad,)))
    sent = up.begin()
    layer_out = back_to_runs(tied(result, sent))
    up.end()
    sent = up.begin(sent)
    back_heads = heads + (to_heads(grad_att),)
    pair_count = back_heads[0].shape[1] // lanes_n
    back = attend(backward_kernel, back_heads, features, 3, head_size, "attend_backward", (sent,))
    if team > 1:
        back = [to_tokens(array) for array in back[:3]]
        back.append(jnp.stack([jnp.sum(back[i].astype(f32), axis=0) for i in (0, 2)]))
    *back, bias_sums = back
    def shard_rows(values):
        return values.reshape(dp_count, -1, qkv_rows).transpose(1, 0, 2).reshape(-1, width)

    side = [shard_rows(bias_sums[:2].reshape(-1)), sums[:6], shard_rows(sums_up[0])]
    side_rows = [part.shape[0] for part in side]
    side_n = -(-sum(side_rows) // lanes_n) * lanes_n
    side.append(jnp.zeros((side_n - sum(side_rows), width), f32))
    wide = Chain([[down_part], up.end(back[0])])
    sent = wide.begin(back[0])
    groups = [(attended, [grad_branch]), (x, back)]
    grads = weight_grads(
        place, groups, jnp.concatenate(side, axis=0), dp_count, (sent, layer_out)
    )
    rest = Scatter(*grads)
    sent = rest.begin()
    result = input_gradient(first, grad_pre, back, (sent,))
    input_grad = back_to_runs(tied(result, sent))
    rest.end(result)
    sent = rest.begin()
    sent = wide.next(sent)
    rest_bits = (ctx_count - 1).bit_length()
    rest = Chain([rest.end(sent)])
    sent = rest.begin(sent)
    while len(wide.plan) > rest_bits + 1:
        sent = wide.next(sent)
    sent = rest.next(sent)
    wide.end(sent)
    pieces = added(wide.parts[0])
    rest.next(pieces, input_grad)
    pieces = lax.all_gather(pieces, "ctx", axis=0)
    while len(rest.plan) > 1:
        rest.next()
    rest.end()
    bits = rest_bits
    pieces = pieces.reshape((2,) * bits + pieces.shape[1:])
    pieces = pieces.transpose(tuple(reversed(range(bits))) + (bits, bits + 1))
    pieces = pieces.reshape(-1, 2 * width).astype(f32)
    down_total = pieces[:, :width]
    up_total = pieces[:, width:].reshape(-1, qkv_rows, width).transpose(1, 0, 2)
    up_total = up_total.reshape(qkv_rows, -1)
    total = rest.parts[0][0].astype(f32)
    out_total, qkv_total = total[:, :width], total[:, width : width + qkv_cols]
    flat = total[:, width + qkv_cols : width + qkv_cols + sum(side_rows)].T
    starts = [0, 2, 3, 4, 8, 5, 6, 7]
    vec_totals = [
        flat[start : start + size // qkv_rows].reshape(-1) for start, size in zip(starts, sizes)
    ]
    return (
        layer_out,
        input_grad,
        qkv_total,
        vec_totals[0],
        out_total,
        vec_totals[1],
        vec_totals[2],
        vec_totals[3],
        up_total,
        vec_totals[4],
        down_total,
        vec_totals[5],
        vec_totals[6],
        vec_totals[7],
    )


def solution(mesh):
    tokens = P("dp", "ctx", None)
    matrix, vector = P("dp", None), P("dp")
    weights = (matrix, vector, matrix, vector, vector, vector, matrix, vector, matrix, vector, vector, vector)
    return jax.shard_map(
        body,
        mesh=mesh,
        in_specs=(tokens, matrix, P("dp", "ctx", None, None), tokens) + weights,
        out_specs=(tokens, tokens) + weights,
        check_vma=False,
    )
```

profile of v0, /device:TPU:0, one launch (start us, length us, event | category | flops | bytes accessed | tf_op | source)
XLA Modules:
  0.0 428.8 jit_solution(13914176525885852802)
XLA Ops:
  7.2 2.3 pack_weights.1
  9.6 3.5 join_weights.1
  13.1 7.3 %all-to-all-start = ((bf16[8,128,768]{2,1,0:T(8,128)(2,1)}), bf16[8,128,768]{2,1,0:T(8,128)(2,1)S(1)}, u32[]{:S(2)}, u32[]{:S(2)}) async-start(bf16[8,128,768]{2,1,0:T(8,128)(2,1)} %param.16), calls=%async_computation | async-start | bytes 3145728 | tf_op jit(solution)/shard_map/all_to_all | solution.py:25
  21.3 36.2 %all-to-all-done = bf16[8,128,768]{2,1,0:T(8,128)(2,1)S(1)} async-done(((bf16[8,128,768]{2,1,0:T(8,128)(2,1)}), bf16[8,128,768]{2,1,0:T(8,128)(2,1)S(1)}, u32[]{:S(2)}, u32[]{:S(2)}) %all-to-all-start) | async-done | bytes 1572896 | tf_op jit(solution)/shard_map/all_to_all | solution.py:25
  57.4 1.1 copy-done.2
  58.6 3.6 all-to-all-start.1
  62.2 2.7 copied.1
  64.9 3.7 all-to-all-done.1
  68.6 3.6 all-to-all-start.2
  72.6 1.1 select_convert_fusion
  78.4 7.7 %project.1 = (bf16[1024,768]{1,0:T(8,128)(2,1)}, bf16[1024,768]{1,0:T(8,128)(2,1)}, bf16[1024,768]{1,0:T(8,128)(2,1)}) custom-call(bf16[1024,768]{1,0:T(8,128)(2,1)} %bitcast.56, bf16[4,208,2304]{2,1,0:T(8,128)(2,1)} %bitcast.63, f32[1,1536]{1,0:T(1,128)} %convert.5.bias_ref), custom_call_target="tpu_custom_call" | custom-call | bytes 1024 | tf_op jit(solution)/shard_map/project/pallas_call | solution.py:421
  87.6 20.3 %attend_forward.1.attended_ref.refs_0_ = bf16[1024,768]{1,0:T(8,128)(2,1)} custom-call(bf16[1024,768]{1,0:T(8,128)(2,1)} %get-tuple-element.35.refs_0_, bf16[1024,768]{1,0:T(8,128)(2,1)} %get-tuple-element.36.refs_1_, bf16[1024,768]{1,0:T(8,128)(2,1)} %get-tuple-element.37.refs_2_, bf16[1024,128]{1,0:T(8,128)(2,1)} %get-tuple-element.89.refs_3_.refs_4_, ...), custom_call_target="tpu_custom_call" | custom-call | bytes 1024 | tf_op jit(solution)/shard_map/attend_forward/pallas_call | solution.py:345
  108.5 9.4 %all-gather.9.cloned.1.call-done = bf16[768,6912]{1,0:T(8,128)(2,1)} async-done(((bf16[192,6912]{1,0:T(8,128)(2,1)}), bf16[768,6912]{1,0:T(8,128)(2,1)}) %all-gather.9.cloned.1.call-update) | async-done | bytes 10616848 | tf_op jit(solution)/shard_map/all_gather | solution.py:799
  117.9 38.4 %token_parts.1 = (bf16[1024,768]{1,0:T(8,128)(2,1)}, bf16[1024,768]{1,0:T(8,128)(2,1)}, bf16[1024,3072]{1,0:T(8,128)(2,1)}, bf16[1024,768]{1,0:T(8,128)(2,1)}, b...) custom-call(bf16[1024,768]{1,0:T(8,128)(2,1)} %attend_forward.1.atte, ...), custom_call_target="tpu_custom_call" | custom-call | bytes 1024 | tf_op jit(solution)/shard_map/token_parts/pallas_call | solution.py:719
  156.3 9.2 %matrix_grad.1.refs_0_ = bf16[3072,768]{1,0:T(8,128)(2,1)} custom-call(bf16[1024,3072]{1,0:T(8,128)(2,1)} %get-tuple-element.41.left_ref, bf16[1024,768]{1,0:T(8,128)(2,1)} %get-tuple-element.42.right_ref), custom_call_target="tpu_custom_call" | custom-call | bytes 768 | tf_op jit(solution)/shard_map/matrix_grad/pallas_call | solution.py:528
  165.5 10.6 %wide_grad.1 = (bf16[1536,768]{1,0:T(8,128)(2,1)}, bf16[1536,768]{1,0:T(8,128)(2,1)}) custom-call(s32[1]{0:T(128)} %bitcast.9.place_ref, bf16[1024,768]{1,0:T(8,128)(2,1)} %get-tuple-element.39.left_ref, bf16[1024,3072]{1,0:T(8,128)(2,1)} %get-tuple-element.40.right_ref, bf16[3072,768]{1,0:T(8,128)(2,1)} %matrix_grad.1.refs_0_), custom_call_target="tpu_custom_call" | custom-call | bytes 768 | tf_op jit(solution)/shard_map/wide_grad/pallas_call | solution.py:498
  176.4 6.0 %all-to-all-start.3 = ((bf16[8,128,768]{2,1,0:T(8,128)(2,1)}), bf16[8,128,768]{2,1,0:T(8,128)(2,1)S(1)}, u32[]{:S(2)}, u32[]{:S(2)}) async-start(bf16[8,128,768]{2,1,0:T(8,128)(2,1)} %bitcast.70), calls=%async_computation.3 | async-start | bytes 3145728 | tf_op jit(solution)/shard_map/all_to_all | solution.py:25
  182.4 4.0 add_convert_fusion.2
  187.2 0.9 slice_reduce_fusion.6
  188.3 47.9 %attend_backward.1 = (bf16[1024,768]{1,0:T(8,128)(2,1)}, bf16[1024,768]{1,0:T(8,128)(2,1)}, bf16[1024,768]{1,0:T(8,128)(2,1)}, f32[8,768]{1,0:T(8,128)}) custom-call(bf16[1024,768]{1,0:T(8,128)(2,1)} %get-tuple-element.35.refs_0_, bf16[1024,768]{1,0:T(8,128)(2,1)} %get-tuple-element.36.refs_1_, bf16[1024,768]{1,0:T(8,128)(2,1)} %get-tuple-element.37.refs_2_, ...), custom_call_target="tpu_custom_call" | custom-call | bytes 1024 | tf_op jit(solution)/shard_map/attend_backward/pallas_call | solution.py:345
  237.1 0.9 maximum_maximum_fusion.refs_6_
  237.9 2.3 add_convert_fusion.8
  240.3 2.2 constant_dynamic-slice_fusion
  242.5 1.1 pad_maximum_fusion.refs_0_
  243.6 1.1 copy-done.3
  244.7 11.9 %weight_grads.1 = (bf16[384,3200]{1,0:T(8,128)(2,1)}, bf16[384,3200]{1,0:T(8,128)(2,1)}) custom-call(s32[1]{0:T(128)} %bitcast.9.place_ref, bf16[1024,768]{1,0:T(8,128)(2,1)} %attend_forward.1.attended_ref.refs_0_, bf16[1024,768]{1,0:T(8,128)(2,1)} %get-tuple-element.50.refs_1_, bf16[1024,768]{1,0:T(8,128)(2,1)} %bitcast.58, ...), custom_call_target="tpu_custom_call" | custom-call | bytes 3200 | tf_op jit(solution)/shard_map/weight_grads/pallas_call | solution.py:474
  256.6 1.3 copy-done.7
  257.9 2.0 collective-permute-start.4
  259.9 8.7 %input_gradient.1.refs_0_.refs_1_ = bf16[1024,768]{1,0:T(8,128)(2,1)} custom-call(bf16[4,208,2304]{2,1,0:T(8,128)(2,1)} %bitcast.65, f32[1024,768]{1,0:T(8,128)} %get-tuple-element.44.refs_1_, bf16[1024,768]{1,0:T(8,128)(2,1)} %get-tuple-element.47.refs_1_.refs_3_.refs_2_, bf16[1024,768]{1,0:T(8,128)(2,1)} %get-tuple-element.48.refs_4_.refs_3_, ...), custom_call_target="tpu_custom_call" | custom-call | bytes 1024 | tf_op jit(solution)/shard_map/input_gradient/pallas_call | solution.py:561
  268.7 4.4 %add_convert_fusion.1 = (bf16[192,3200]{1,0:T(8,128)(2,1)}, bf16[192,3200]{1,0:T(8,128)(2,1)}) fusion(bf16[384,3200]{1,0:T(8,128)(2,1)} %tied.28, bf16[384,3200]{1,0:T(8,128)(2,1)} %get-tuple-element.55), kind=kLoop, calls=%fused_computation.2 | loop fusion | flops 4915200 | bytes 7372800 | tf_op jit(solution)/shard_map/convert_element_type | solution.py:60
  273.0 1.5 collective-permute-start.3
  274.6 4.5 %all-to-all-start.4 = ((bf16[8,128,768]{2,1,0:T(8,128)(2,1)}), bf16[8,128,768]{2,1,0:T(8,128)(2,1)S(1)}, u32[]{:S(2)}, u32[]{:S(2)}) async-start(bf16[8,128,768]{2,1,0:T(8,128)(2,1)} %bitcast.59), calls=%async_computation.5 | async-start | bytes 3145728 | tf_op jit(solution)/shard_map/all_to_all | solution.py:25
  279.1 17.0 %collective-permute-done.4 = bf16[384,1536]{1,0:T(8,128)(2,1)} collective-permute-done((bf16[384,1536]{1,0:T(8,128)(2,1)S(1)}, bf16[384,1536]{1,0:T(8,128)(2,1)}, u32[]{:S(2)}, u32[]{:S(2)}) %collective-permute-start.4) | collective-permute-done | bytes 1179680 | tf_op jit(solution)/shard_map/ppermute | solution.py:97
  296.1 2.7 add_convert_fusion.6
  298.9 2.5 collective-permute-done.3.refs_0_
  301.4 2.4 add_convert_fusion.5
  303.8 1.5 collective-permute-start.5
  305.3 13.3 %collective-permute-done.6 = bf16[192,1536]{1,0:T(8,128)(2,1)} collective-permute-done((bf16[192,1536]{1,0:T(8,128)(2,1)}, bf16[192,1536]{1,0:T(8,128)(2,1)}, u32[]{:S(2)}, u32[]{:S(2)}) %collective-permute-start.6) | collective-permute-done | bytes 589856 | tf_op jit(solution)/shard_map/ppermute | solution.py:97
  318.6 1.7 add_convert_fusion.14.refs_0_
  320.4 2.3 collective-permute-start.8
  322.6 1.9 add_convert_fusion.11
  324.6 1.2 collective-permute-start.7
  325.8 8.3 %collective-permute-done.8.refs_0_ = bf16[96,1536]{1,0:T(8,128)(2,1)S(1)} collective-permute-done((bf16[96,1536]{1,0:T(8,128)(2,1)}, bf16[96,1536]{1,0:T(8,128)(2,1)S(1)}, u32[]{:S(2)}, u32[]{:S(2)}) %collective-permute-start.8) | collective-permute-done | bytes 294944 | tf_op jit(solution)/shard_map/ppermute | solution.py:97
  334.8 1.9 add_convert_fusion.12.refs_1_
  338.1 1.1 copy-done.5
  339.2 7.3 %collective-permute-done.9 = bf16[24,3200]{1,0:T(8,128)(2,1)S(1)} collective-permute-done((bf16[24,3200]{1,0:T(8,128)(2,1)}, bf16[24,3200]{1,0:T(8,128)(2,1)S(1)}, u32[]{:S(2)}, u32[]{:S(2)}) %collective-permute-start.9) | collective-permute-done | bytes 153632 | tf_op jit(solution)/shard_map/ppermute | solution.py:97
  347.3 7.4 %collective-permute-done.10 = bf16[24,3200]{1,0:T(8,128)(2,1)S(1)} collective-permute-done((bf16[24,3200]{1,0:T(8,128)(2,1)}, bf16[24,3200]{1,0:T(8,128)(2,1)S(1)}, u32[]{:S(2)}, u32[]{:S(2)}) %collective-permute-start.10) | collective-permute-done | bytes 153632 | tf_op jit(solution)/shard_map/ppermute | solution.py:97
  354.7 0.9 broadcast_select_fusion.5
  356.4 8.4 %collective-permute-done.11 = bf16[48,3200]{1,0:T(8,128)(2,1)S(1)} collective-permute-done((bf16[48,3200]{1,0:T(8,128)(2,1)}, bf16[48,3200]{1,0:T(8,128)(2,1)S(1)}, u32[]{:S(2)}, u32[]{:S(2)}) %collective-permute-start.11) | collective-permute-done | bytes 307232 | tf_op jit(solution)/shard_map/ppermute | solution.py:97
  364.8 1.0 broadcast_select_fusion.3
  365.9 0.9 pad_maximum_fusion.1.refs_0_
  366.7 5.1 %collective-permute-start.12 = (bf16[96,3200]{1,0:T(8,128)(2,1)}, bf16[96,3200]{1,0:T(8,128)(2,1)S(1)}, u32[]{:S(2)}, u32[]{:S(2)}) collective-permute-start(bf16[96,3200]{1,0:T(8,128)(2,1)} %tied.39), channel_id=1, source_target_pairs={{0,1},{1,0},{2,3},{3,2},{4,5},{5,4},{6,7},{7,6},{8,9},{9,8},{10,11... | collective-permute-start | bytes 1843208 | tf_op jit(solution)/shard_map/ppermute | solution.py:97
  371.8 13.6 %collective-permute-done.12 = bf16[96,3200]{1,0:T(8,128)(2,1)S(1)} collective-permute-done((bf16[96,3200]{1,0:T(8,128)(2,1)}, bf16[96,3200]{1,0:T(8,128)(2,1)S(1)}, u32[]{:S(2)}, u32[]{:S(2)}) %collective-permute-start.12) | collective-permute-done | bytes 614432 | tf_op jit(solution)/shard_map/ppermute | solution.py:97
  385.4 1.2 broadcast_select_fusion.1
  388.4 1.3 slice.133
  389.7 1.1 slice_reduce_fusion
  390.7 0.9 maximum_convert_fusion.1
  391.6 20.9 %all-gather.11.cloned.1.call-done = bf16[768,1536]{1,0:T(8,128)(2,1)} async-done(((bf16[96,1536]{1,0:T(8,128)(2,1)}), bf16[768,1536]{1,0:T(8,128)(2,1)}) %all-gather.11.cloned.1.call-update) | async-done | bytes 2359312 | tf_op jit(solution)/shard_map/all_gather | solution.py:889
  412.5 2.3 convert_bitcast_fusion
  415.1 1.8 fusion.10
  416.9 1.7 copy.77
  418.7 1.1 copy.104
  419.8 0.8 copy-done.6
  420.7 1.1 copy.105
  (126 shorter events, 16.3 us)
Async XLA Ops:
  7.2 65.3 %copy-start = (s32[8,1024]{1,0:T(8,128)S(1)}, s32[8,1024]{1,0:T(8,128)}, u32[]{:S(2)}) copy-start(s32[8,1024]{1,0:T(8,128)} %param.17) | copy-start | bytes 98308
  7.2 69.0 %all-gather.7.cloned.1.call-start = ((), (), s32[]{:S(2)}) async-start(), calls=%async_computation.7 | async-start | bytes 4792320 | tf_op jit(solution)/shard_map/all_gather | solution.py:798
  9.5 108.3 %all-gather.9.cloned.1.call-start = ((), (), s32[]{:S(2)}) async-start(), calls=%async_computation.8 | async-start | bytes 13271040 | tf_op jit(solution)/shard_map/all_gather | solution.py:799
  13.1 7.3 %copy-start.13 = (s32[8,2,12,3]{2,1,3,0:T(2,128)S(1)}, s32[8,2,12,3]{2,1,3,0:T(2,128)}, u32[]{:S(2)}) copy-start(s32[8,2,12,3]{2,1,3,0:T(2,128)} %param.18) | copy-start | bytes 6916
  13.1 44.3 %all-to-all-start = ((bf16[8,128,768]{2,1,0:T(8,128)(2,1)}), bf16[8,128,768]{2,1,0:T(8,128)(2,1)S(1)}, u32[]{:S(2)}, u32[]{:S(2)}) async-start(bf16[8,128,768]{2,1,0:T(8,128)(2,1)} %param.16), calls=%async_computation | async-start | bytes 3145728 | tf_op jit(solution)/shard_map/all_to_all | solution.py:25
  57.4 1.1 copy-start.2
  58.6 10.0 %all-to-all-start.1 = ((s32[8,1,72]{2,1,0:T(1,128)}), s32[8,1,72]{2,1,0:T(1,128)S(1)}, u32[]{:S(2)}, u32[]{:S(2)}) async-start(s32[8,1,72]{2,1,0:T(1,128)} %tied.20), calls=%async_computation.1 | async-start | bytes 8192 | tf_op jit(solution)/shard_map/all_to_all | solution.py:25
  68.6 39.9 %all-to-all-start.2 = ((bf16[8,128,768]{2,1,0:T(8,128)(2,1)}), bf16[8,128,768]{2,1,0:T(8,128)(2,1)S(1)}, u32[]{:S(2)}, u32[]{:S(2)}) async-start(bf16[8,128,768]{2,1,0:T(8,128)(2,1)} %copied.1), calls=%async_computation.2 | async-start | bytes 3145728 | tf_op jit(solution)/shard_map/all_to_all | solution.py:25
  72.2 168.1 %reduce-scatter.2.cloned.1.call-start = ((), (), s32[]{:S(2)}) async-start(), calls=%async_computation.6 | async-start | bytes 5898240 | tf_op jit(solution)/shard_map/reduce_scatter | solution.py:155
  108.5 9.4 %copy-start.8 = (bf16[8,128,768]{2,1,0:T(8,128)(2,1)}, bf16[8,128,768]{2,1,0:T(8,128)(2,1)S(1)}, u32[]{:S(2)}) copy-start(bf16[8,128,768]{2,1,0:T(8,128)(2,1)S(1)} %all-to-all-done.2) | copy-start | bytes 4718596
  176.1 6.3 %collective-permute-start = (bf16[1536,768]{1,0:T(8,128)(2,1)}, bf16[1536,768]{1,0:T(8,128)(2,1)}, u32[]{:S(2)}, u32[]{:S(2)}) collective-permute-start(bf16[1536,768]{1,0:T(8,128)(2,1)} %tied.21.refs_1_), channel_id=1, source_target_pairs={{0,8},{8,0},{16,24},{24,16},{1,9},{9,1},{17,25},{25,17},{2,10},{10... | collective-permute-start | bytes 7077896 | tf_op jit(solution)/shard_map/ppermute | solution.py:127
  176.4 67.2 %all-to-all-start.3 = ((bf16[8,128,768]{2,1,0:T(8,128)(2,1)}), bf16[8,128,768]{2,1,0:T(8,128)(2,1)S(1)}, u32[]{:S(2)}, u32[]{:S(2)}) async-start(bf16[8,128,768]{2,1,0:T(8,128)(2,1)} %bitcast.70), calls=%async_computation.3 | async-start | bytes 3145728 | tf_op jit(solution)/shard_map/all_to_all | solution.py:25
  186.4 51.5 %collective-permute-start.1 = (bf16[768,768]{1,0:T(8,128)(2,1)}, bf16[768,768]{1,0:T(8,128)(2,1)}, u32[]{:S(2)}, u32[]{:S(2)}) collective-permute-start(bf16[768,768]{1,0:T(8,128)(2,1)} %tied.23.refs_7_), channel_id=1, source_target_pairs={{0,16},{8,24},{16,0},{24,8},{1,17},{9,25},{17,1},{25,9},{2,18},{10... | collective-permute-start | bytes 3538952 | tf_op jit(solution)/shard_map/ppermute | solution.py:127
  188.3 48.8 %copy-start.14 = (f32[8,768]{1,0:T(8,128)S(1)}, f32[8,768]{1,0:T(8,128)}, u32[]{:S(2)}) copy-start(f32[8,768]{1,0:T(8,128)} %get-tuple-element.52) | copy-start | bytes 73732
  240.3 2.2 copy-start.11
  243.6 1.1 copy-start.3
  256.6 1.3 copy-start.7
  256.6 12.0 %collective-permute-start.2 = (bf16[384,3200]{1,0:T(8,128)(2,1)}, bf16[384,3200]{1,0:T(8,128)(2,1)}, u32[]{:S(2)}, u32[]{:S(2)}) collective-permute-start(bf16[384,3200]{1,0:T(8,128)(2,1)} %tied.26.refs_5_.refs_1_), channel_id=1, source_target_pairs={{0,8},{8,0},{16,24},{24,16},{1,9},{9,1},{17,25},{25,17},{2,10},{10... | collective-permute-start | bytes 7372808 | tf_op jit(solution)/shard_map/ppermute | solution.py:127
  257.9 38.2 %collective-permute-start.4 = (bf16[384,1536]{1,0:T(8,128)(2,1)S(1)}, bf16[384,1536]{1,0:T(8,128)(2,1)}, u32[]{:S(2)}, u32[]{:S(2)}) collective-permute-start(bf16[384,1536]{1,0:T(8,128)(2,1)S(1)} %copy-done.7), channel_id=1, source_target_pairs={{0,1},{1,0},{2,3},{3,2},{4,5},{5,4},{6,7},{7,6},{8,9},{9,8},{10,11... | collective-permute-start | bytes 3538952 | tf_op jit(solution)/shard_map/ppermute | solution.py:97
  273.0 28.3 %collective-permute-start.3 = (bf16[192,3200]{1,0:T(8,128)(2,1)}, bf16[192,3200]{1,0:T(8,128)(2,1)}, u32[]{:S(2)}, u32[]{:S(2)}) collective-permute-start(bf16[192,3200]{1,0:T(8,128)(2,1)} %tied.29.refs_1_), channel_id=1, source_target_pairs={{0,16},{8,24},{16,0},{24,8},{1,17},{9,25},{17,1},{25,9},{2,18},{10... | collective-permute-start | bytes 3686408 | tf_op jit(solution)/shard_map/ppermute | solution.py:127
  274.6 63.5 %all-to-all-start.4 = ((bf16[8,128,768]{2,1,0:T(8,128)(2,1)}), bf16[8,128,768]{2,1,0:T(8,128)(2,1)S(1)}, u32[]{:S(2)}, u32[]{:S(2)}) async-start(bf16[8,128,768]{2,1,0:T(8,128)(2,1)} %bitcast.59), calls=%async_computation.5 | async-start | bytes 3145728 | tf_op jit(solution)/shard_map/all_to_all | solution.py:25
  279.1 133.4 %all-gather.11.cloned.1.call-start = ((), (), s32[]{:S(2)}) async-start(), calls=%async_computation.9 | async-start | bytes 2654208 | tf_op jit(solution)/shard_map/all_gather | solution.py:889
  298.8 2.6 copy-start.9
  298.8 19.8 %collective-permute-start.6 = (bf16[192,1536]{1,0:T(8,128)(2,1)}, bf16[192,1536]{1,0:T(8,128)(2,1)}, u32[]{:S(2)}, u32[]{:S(2)}) collective-permute-start(bf16[192,1536]{1,0:T(8,128)(2,1)} %tied.30.refs_1_), channel_id=1, source_target_pairs={{0,2},{1,3},{2,0},{3,1},{4,6},{5,7},{6,4},{7,5},{8,10},{9,11},{10,... | collective-permute-start | bytes 1769480 | tf_op jit(solution)/shard_map/ppermute | solution.py:97
  303.8 14.8 %copy-start.10 = (bf16[192,1536]{1,0:T(8,128)(2,1)S(1)}, bf16[192,1536]{1,0:T(8,128)(2,1)}, u32[]{:S(2)}) copy-start(bf16[192,1536]{1,0:T(8,128)(2,1)} %get-tuple-element.70) | copy-start | bytes 1769476
  303.8 18.8 %collective-permute-start.5 = (bf16[96,3200]{1,0:T(8,128)(2,1)}, bf16[96,3200]{1,0:T(8,128)(2,1)}, u32[]{:S(2)}, u32[]{:S(2)}) collective-permute-start(bf16[96,3200]{1,0:T(8,128)(2,1)} %tied.32.refs_1_), channel_id=1, source_target_pairs={{0,1},{1,0},{2,3},{3,2},{4,5},{5,4},{6,7},{7,6},{8,9},{9,8},{10,11... | collective-permute-start | bytes 1843208 | tf_op jit(solution)/shard_map/ppermute | solution.py:97
  320.4 13.7 %collective-permute-start.8 = (bf16[96,1536]{1,0:T(8,128)(2,1)}, bf16[96,1536]{1,0:T(8,128)(2,1)S(1)}, u32[]{:S(2)}, u32[]{:S(2)}) collective-permute-start(bf16[96,1536]{1,0:T(8,128)(2,1)} %tied.33.refs_1_), channel_id=1, source_target_pairs={{0,4},{1,5},{2,6},{3,7},{4,0},{5,1},{6,2},{7,3},{8,12},{9,13},{10,... | collective-permute-start | bytes 884744 | tf_op jit(solution)/shard_map/ppermute | solution.py:97
  324.6 12.8 %collective-permute-start.7 = (bf16[48,3200]{1,0:T(8,128)(2,1)}, bf16[48,3200]{1,0:T(8,128)(2,1)S(1)}, u32[]{:S(2)}, u32[]{:S(2)}) collective-permute-start(bf16[48,3200]{1,0:T(8,128)(2,1)} %tied.34.refs_1_), channel_id=1, source_target_pairs={{0,2},{1,3},{2,0},{3,1},{4,6},{5,7},{6,4},{7,5},{8,10},{9,11},{10,... | collective-permute-start | bytes 921608 | tf_op jit(solution)/shard_map/ppermute | solution.py:97
  334.1 0.7 copy-start.12
  338.1 1.1 copy-start.5
  339.2 7.3 %collective-permute-start.9 = (bf16[24,3200]{1,0:T(8,128)(2,1)}, bf16[24,3200]{1,0:T(8,128)(2,1)S(1)}, u32[]{:S(2)}, u32[]{:S(2)}) collective-permute-start(bf16[24,3200]{1,0:T(8,128)(2,1)} %tied.36), channel_id=1, source_target_pairs={{0,4},{1,5},{2,6},{3,7},{4,0},{5,1},{6,2},{7,3},{8,12},{9,13},{10,... | collective-permute-start | bytes 460808 | tf_op jit(solution)/shard_map/ppermute | solution.py:97
  347.3 7.4 %collective-permute-start.10 = (bf16[24,3200]{1,0:T(8,128)(2,1)}, bf16[24,3200]{1,0:T(8,128)(2,1)S(1)}, u32[]{:S(2)}, u32[]{:S(2)}) collective-permute-start(bf16[24,3200]{1,0:T(8,128)(2,1)} %tied.37), channel_id=1, source_target_pairs={{0,4},{1,5},{2,6},{3,7},{4,0},{5,1},{6,2},{7,3},{8,12},{9,13},{10,... | collective-permute-start | bytes 460808 | tf_op jit(solution)/shard_map/ppermute | solution.py:97
  356.4 8.5 %collective-permute-start.11 = (bf16[48,3200]{1,0:T(8,128)(2,1)}, bf16[48,3200]{1,0:T(8,128)(2,1)S(1)}, u32[]{:S(2)}, u32[]{:S(2)}) collective-permute-start(bf16[48,3200]{1,0:T(8,128)(2,1)} %tied.38), channel_id=1, source_target_pairs={{0,2},{1,3},{2,0},{3,1},{4,6},{5,7},{6,4},{7,5},{8,10},{9,11},{10,... | collective-permute-start | bytes 921608 | tf_op jit(solution)/shard_map/ppermute | solution.py:97
  366.7 18.6 %collective-permute-start.12 = (bf16[96,3200]{1,0:T(8,128)(2,1)}, bf16[96,3200]{1,0:T(8,128)(2,1)S(1)}, u32[]{:S(2)}, u32[]{:S(2)}) collective-permute-start(bf16[96,3200]{1,0:T(8,128)(2,1)} %tied.39), channel_id=1, source_target_pairs={{0,1},{1,0},{2,3},{3,2},{4,5},{5,4},{6,7},{7,6},{8,9},{9,8},{10,11... | collective-permute-start | bytes 1843208 | tf_op jit(solution)/shard_map/ppermute | solution.py:97
  416.9 1.8 copy-start.4
  418.7 2.0 copy-start.6
  418.7 3.1 copy-start.1
Sparse Core Ops, SparseCore 0:
  10.2 35.1 all-gather.6
  46.9 70.9 all-gather.8
  165.6 70.6 reduce-scatter.1
  356.5 55.9 all-gather.10
where the time goes:
time: 435 us; the launch traced here: 429 us
  Pallas kernels  163 us (37%)
  waiting for transfers between devices  149 us (34%)
  starting transfers between devices  39.8 us (9%)
  other arithmetic  37.6 us (9%)
  local copies, waits for them, and re-layouts  25.1 us (6%)
  between operations  14.5 us (3%)
    ppermute x9, waiting for transfers between devices, begin(): lax.ppermute(sent, self.axis, [(i, i ^ stride) for i in range(size)])  76 us
    pallas_call x2, Pallas kernels, attend(): pl.pallas_call(run, grid=(count,), in_specs=[pair] * len(arrays) + [whole...  68.1 us
    all_to_all x5, waiting for transfers between devices, swap_pieces(): lax.all_to_all(pieces, axis, 0, 0, axis_index_groups=groups, tiled=True)  39.9 us
    pallas_call x1, Pallas kernels, token_parts(): pl.pallas_call(token_kernel, grid=(tokens // tile,), in_specs=[row(width)...  38.4 us
    all_to_all x5, starting transfers between devices, swap_pieces(): lax.all_to_all(pieces, axis, 0, 0, axis_index_groups=groups, tiled=True)  25 us
    convert_element_type x10, other arithmetic, added(): return total.astype(bf16)  22.8 us
    all_gather x1, waiting for transfers between devices, body(): pieces = lax.all_gather(pieces, 'ctx', axis=0)  20.9 us
    ppermute x9, starting transfers between devices, begin(): lax.ppermute(sent, self.axis, [(i, i ^ stride) for i in range(size)])  12.2 us
  transfers between devices with their start and end apart: 22, of which 13 were waited for; matrix products, arithmetic and copies ran while one was open for 11% of the time, Pallas kernels for 24%

commit v1 on v0

--- a/solution.py
+++ b/solution.py
@@ -1,4 +1,5 @@
 import functools
+import math
 
 import jax
 import jax.numpy as jnp
@@ -535,6 +536,36 @@
         cost_estimate=pl.CostEstimate(flops=0, bytes_accessed=cols, transcendentals=0),
         name="matrix_grad",
     )(left, right, *after)
+
+
+def spread_kernel(pieces_ref, down_ref, up_ref):
+    count, rows, cols = pieces_ref.shape
+    width = cols // 2
+    part = up_ref.shape[0]
+    bits = (count - 1).bit_length()
+    for device in range(count):
+        place = sum(((device >> bit) & 1) << (bits - 1 - bit) for bit in range(bits))
+        piece = pieces_ref[device].astype(f32)
+        down_ref[place * rows : (place + 1) * rows, :] = piece[:, :width]
+        for start in range(0, rows, math.gcd(rows, part)):
+            size = math.gcd(rows, part)
+            run, row = divmod(place * rows + start, part)
+            cells = piece[start : start + size, width:]
+            up_ref[row : row + size, run * width : (run + 1) * width] = cells
+
+
+def spread_gradients(pieces, part):
+    count, rows, cols = pieces.shape
+    width = cols // 2
+    return pl.pallas_call(
+        spread_kernel,
+        out_shape=[
+            jax.ShapeDtypeStruct((count * rows, width), f32),
+            jax.ShapeDtypeStruct((part, count * rows // part * width), f32),
+        ],
+        compiler_params=pltpu.CompilerParams(vmem_limit_bytes=vmem_cap),
+        name="spread_gradients",
+    )(pieces)
 
 
 def input_kernel(*refs, part, parts_n):
@@ -882,21 +913,17 @@
     sent = rest.begin(sent)
     while len(wide.plan) > rest_bits + 1:
         sent = wide.next(sent)
+    layer_out = copied(layer_out, sent)
     sent = rest.next(sent)
     wide.end(sent)
     pieces = added(wide.parts[0])
     rest.next(pieces, input_grad)
     pieces = lax.all_gather(pieces, "ctx", axis=0)
     while len(rest.plan) > 1:
-        rest.next()
+        sent = rest.next()
+    input_grad = copied(input_grad, sent)
     rest.end()
-    bits = rest_bits
-    pieces = pieces.reshape((2,) * bits + pieces.shape[1:])
-    pieces = pieces.transpose(tuple(reversed(range(bits))) + (bits, bits + 1))
-    pieces = pieces.reshape(-1, 2 * width).astype(f32)
-    down_total = pieces[:, :width]
-    up_total = pieces[:, width:].reshape(-1, qkv_rows, width).transpose(1, 0, 2)
-    up_total = up_total.reshape(qkv_rows, -1)
+    down_total, up_total = spread_gradients(pieces, qkv_rows)
     total = rest.parts[0][0].astype(f32)
     out_total, qkv_total = total[:, :width], total[:, width : width + qkv_cols]
     flat = total[:, width + qkv_cols : width + qkv_cols + sum(side_rows)].T

time: 435 us -> 432 us (level)
  Pallas kernels: 163 us -> 173 us
  local copies, waits for them, and re-layouts: 25.1 us -> 18.1 us
    pallas_call x1 -> x3, Pallas kernels: 2.65 us -> 8.03 us  [copied(): pl.pallas_call(copy, in_specs=[pl.BlockSpec(memory_space=pltpu.VMEM)] + [...]
    ppermute x9, waiting for transfers between devices: 76 us -> 71.6 us  [begin(): lax.ppermute(sent, self.axis, [(i, i ^ stride) for i in range(size)])]
    unnamed x33 -> x31, local copies, waits for them, and re-layouts: 8.79 us -> 5.57 us
  transfers between devices with their start and end apart: 22 -> 22, of which waited for: 13 -> 13; matrix products, arithmetic and copies ran while one was open for 11% -> 11% of each run, Pallas kernels for 24% -> 25%
where the time goes in v1:
time: 432 us; the launch traced here: 425 us
  Pallas kernels  173 us (40%)
  waiting for transfers between devices  146 us (34%)
  starting transfers between devices  39.6 us (9%)
  other arithmetic  34.5 us (8%)
  local copies, waits for them, and re-layouts  18.1 us (4%)
  between operations  14.5 us (3%)
    ppermute x9, waiting for transfers between devices, begin(): lax.ppermute(sent, self.axis, [(i, i ^ stride) for i in range(size)])  71.6 us
    pallas_call x2, Pallas kernels, attend(): pl.pallas_call(run, grid=(count,), in_specs=[pair] * len(arrays) + [whole...  68.1 us
    all_to_all x5, waiting for transfers between devices, swap_pieces(): lax.all_to_all(pieces, axis, 0, 0, axis_index_groups=groups, tiled=True)  39.9 us
    pallas_call x1, Pallas kernels, token_parts(): pl.pallas_call(token_kernel, grid=(tokens // tile,), in_specs=[row(width)...  38.4 us
    all_to_all x5, starting transfers between devices, swap_pieces(): lax.all_to_all(pieces, axis, 0, 0, axis_index_groups=groups, tiled=True)  25.1 us
    convert_element_type x10, other arithmetic, added(): return total.astype(bf16)  23.1 us
    all_gather x1, waiting for transfers between devices, body(): pieces = lax.all_gather(pieces, 'ctx', axis=0)  22.2 us
    pallas_call x1, Pallas kernels, weight_grads(): pl.pallas_call(functools.partial(grads_kernel, groups=places, held=held,...  11.9 us
  transfers between devices with their start and end apart: 22, of which 13 were waited for; matrix products, arithmetic and copies ran while one was open for 11% of the time, Pallas kernels for 25%

profile of v1, /device:TPU:0, one launch (start us, length us, event | category | flops | bytes accessed | tf_op | source)
XLA Modules:
  0.0 424.8 jit_solution(6891702541852392658)
XLA Ops:
  7.2 2.3 pack_weights.1
  9.6 3.5 join_weights.1
  13.1 7.3 %all-to-all-start = ((bf16[8,128,768]{2,1,0:T(8,128)(2,1)}), bf16[8,128,768]{2,1,0:T(8,128)(2,1)S(1)}, u32[]{:S(2)}, u32[]{:S(2)}) async-start(bf16[8,128,768]{2,1,0:T(8,128)(2,1)} %param.16), calls=%async_computation | async-start | bytes 3145728 | tf_op jit(solution)/shard_map/all_to_all | solution.py:26
  21.3 36.2 %all-to-all-done = bf16[8,128,768]{2,1,0:T(8,128)(2,1)S(1)} async-done(((bf16[8,128,768]{2,1,0:T(8,128)(2,1)}), bf16[8,128,768]{2,1,0:T(8,128)(2,1)S(1)}, u32[]{:S(2)}, u32[]{:S(2)}) %all-to-all-start) | async-done | bytes 1572896 | tf_op jit(solution)/shard_map/all_to_all | solution.py:26
  57.4 1.1 copy-done.2
  58.6 3.6 all-to-all-start.1
  62.2 2.7 copied.3
  64.9 3.7 all-to-all-done.1
  68.6 3.6 all-to-all-start.2
  72.6 1.1 select_convert_fusion
  75.5 0.8 maximum_maximum_fusion.1.refs_5_.refs_6_
  76.2 0.7 slice.116
  77.0 0.8 slice.120
  78.4 7.7 %project.1 = (bf16[1024,768]{1,0:T(8,128)(2,1)}, bf16[1024,768]{1,0:T(8,128)(2,1)}, bf16[1024,768]{1,0:T(8,128)(2,1)}) custom-call(bf16[1024,768]{1,0:T(8,128)(2,1)} %bitcast.47, bf16[4,208,2304]{2,1,0:T(8,128)(2,1)} %bitcast.53, f32[1,1536]{1,0:T(1,128)} %convert.2.bias_ref), custom_call_target="tpu_custom_call" | custom-call | bytes 1024 | tf_op jit(solution)/shard_map/project/pallas_call | solution.py:422
  87.6 20.3 %attend_forward.1.attended_ref.refs_0_ = bf16[1024,768]{1,0:T(8,128)(2,1)} custom-call(bf16[1024,768]{1,0:T(8,128)(2,1)} %get-tuple-element.37.refs_0_, bf16[1024,768]{1,0:T(8,128)(2,1)} %get-tuple-element.38.refs_1_, bf16[1024,768]{1,0:T(8,128)(2,1)} %get-tuple-element.39.refs_2_, bf16[1024,128]{1,0:T(8,128)(2,1)} %get-tuple-element.91.refs_3_.refs_4_, ...), custom_call_target="tpu_custom_call" | custom-call | bytes 1024 | tf_op jit(solution)/shard_map/attend_forward/pallas_call | solution.py:346
  108.5 9.4 %all-gather.9.cloned.1.call-done = bf16[768,6912]{1,0:T(8,128)(2,1)} async-done(((bf16[192,6912]{1,0:T(8,128)(2,1)}), bf16[768,6912]{1,0:T(8,128)(2,1)}) %all-gather.9.cloned.1.call-update) | async-done | bytes 10616848 | tf_op jit(solution)/shard_map/all_gather | solution.py:830
  117.9 38.4 %token_parts.1 = (bf16[1024,768]{1,0:T(8,128)(2,1)}, bf16[1024,768]{1,0:T(8,128)(2,1)}, bf16[1024,3072]{1,0:T(8,128)(2,1)}, bf16[1024,768]{1,0:T(8,128)(2,1)}, b...) custom-call(bf16[1024,768]{1,0:T(8,128)(2,1)} %attend_forward.1.atte, ...), custom_call_target="tpu_custom_call" | custom-call | bytes 1024 | tf_op jit(solution)/shard_map/token_parts/pallas_call | solution.py:750
  156.3 9.2 %matrix_grad.1.refs_0_ = bf16[3072,768]{1,0:T(8,128)(2,1)} custom-call(bf16[1024,3072]{1,0:T(8,128)(2,1)} %get-tuple-element.43.left_ref, bf16[1024,768]{1,0:T(8,128)(2,1)} %get-tuple-element.44.right_ref), custom_call_target="tpu_custom_call" | custom-call | bytes 768 | tf_op jit(solution)/shard_map/matrix_grad/pallas_call | solution.py:529
  165.5 10.6 %wide_grad.1 = (bf16[1536,768]{1,0:T(8,128)(2,1)}, bf16[1536,768]{1,0:T(8,128)(2,1)}) custom-call(s32[1]{0:T(128)} %bitcast.9.place_ref, bf16[1024,768]{1,0:T(8,128)(2,1)} %get-tuple-element.41.left_ref, bf16[1024,3072]{1,0:T(8,128)(2,1)} %get-tuple-element.42.right_ref, bf16[3072,768]{1,0:T(8,128)(2,1)} %matrix_grad.1.refs_0_), custom_call_target="tpu_custom_call" | custom-call | bytes 768 | tf_op jit(solution)/shard_map/wide_grad/pallas_call | solution.py:499
  176.4 6.0 %all-to-all-start.3 = ((bf16[8,128,768]{2,1,0:T(8,128)(2,1)}), bf16[8,128,768]{2,1,0:T(8,128)(2,1)S(1)}, u32[]{:S(2)}, u32[]{:S(2)}) async-start(bf16[8,128,768]{2,1,0:T(8,128)(2,1)} %bitcast.59), calls=%async_computation.3 | async-start | bytes 3145728 | tf_op jit(solution)/shard_map/all_to_all | solution.py:26
  182.4 4.0 add_convert_fusion.3
  187.2 0.9 slice_reduce_fusion.6
  188.3 47.9 %attend_backward.1 = (bf16[1024,768]{1,0:T(8,128)(2,1)}, bf16[1024,768]{1,0:T(8,128)(2,1)}, bf16[1024,768]{1,0:T(8,128)(2,1)}, f32[8,768]{1,0:T(8,128)}) custom-call(bf16[1024,768]{1,0:T(8,128)(2,1)} %get-tuple-element.37.refs_0_, bf16[1024,768]{1,0:T(8,128)(2,1)} %get-tuple-element.38.refs_1_, bf16[1024,768]{1,0:T(8,128)(2,1)} %get-tuple-element.39.refs_2_, ...), custom_call_target="tpu_custom_call" | custom-call | bytes 1024 | tf_op jit(solution)/shard_map/attend_backward/pallas_call | solution.py:346
  237.1 0.9 maximum_maximum_fusion.refs_6_
  237.9 2.5 add_convert_fusion.8
  240.5 2.2 constant_dynamic-slice_fusion
  242.7 1.1 pad_maximum_fusion.refs_0_
  243.8 1.1 copy-done.4
  244.9 11.9 %weight_grads.1 = (bf16[384,3200]{1,0:T(8,128)(2,1)}, bf16[384,3200]{1,0:T(8,128)(2,1)}) custom-call(s32[1]{0:T(128)} %bitcast.9.place_ref, bf16[1024,768]{1,0:T(8,128)(2,1)} %attend_forward.1.attended_ref.refs_0_, bf16[1024,768]{1,0:T(8,128)(2,1)} %get-tuple-element.49.refs_1_, bf16[1024,768]{1,0:T(8,128)(2,1)} %bitcast.49, ...), custom_call_target="tpu_custom_call" | custom-call | bytes 3200 | tf_op jit(solution)/shard_map/weight_grads/pallas_call | solution.py:475
  256.8 1.3 copy-done.5
  258.1 2.0 collective-permute-start.2
  260.1 8.7 %input_gradient.1.refs_1_.refs_0_ = bf16[1024,768]{1,0:T(8,128)(2,1)} custom-call(bf16[4,208,2304]{2,1,0:T(8,128)(2,1)} %bitcast.55, f32[1024,768]{1,0:T(8,128)} %get-tuple-element.57.refs_1_, bf16[1024,768]{1,0:T(8,128)(2,1)} %get-tuple-element.48.refs_1_.refs_3_.refs_2_, bf16[1024,768]{1,0:T(8,128)(2,1)} %get-tuple-element.50.refs_4_.refs_3_, ...), custom_call_target="tpu_custom_call" | custom-call | bytes 1024 | tf_op jit(solution)/shard_map/input_gradient/pallas_call | solution.py:592
  268.8 4.4 %add_convert_fusion = (bf16[192,3200]{1,0:T(8,128)(2,1)}, bf16[192,3200]{1,0:T(8,128)(2,1)}) fusion(bf16[384,3200]{1,0:T(8,128)(2,1)} %tied.27, bf16[384,3200]{1,0:T(8,128)(2,1)} %get-tuple-element.55), kind=kLoop, calls=%fused_computation | loop fusion | flops 4915200 | bytes 7372800 | tf_op jit(solution)/shard_map/convert_element_type | solution.py:61
  273.2 1.5 collective-permute-start.5
  274.8 4.6 %all-to-all-start.4 = ((bf16[8,128,768]{2,1,0:T(8,128)(2,1)}), bf16[8,128,768]{2,1,0:T(8,128)(2,1)S(1)}, u32[]{:S(2)}, u32[]{:S(2)}) async-start(bf16[8,128,768]{2,1,0:T(8,128)(2,1)} %bitcast.50), calls=%async_computation.5 | async-start | bytes 3145728 | tf_op jit(solution)/shard_map/all_to_all | solution.py:26
  279.5 16.8 %collective-permute-done.2 = bf16[384,1536]{1,0:T(8,128)(2,1)} collective-permute-done((bf16[384,1536]{1,0:T(8,128)(2,1)S(1)}, bf16[384,1536]{1,0:T(8,128)(2,1)}, u32[]{:S(2)}, u32[]{:S(2)}) %collective-permute-start.2) | collective-permute-done | bytes 1179680 | tf_op jit(solution)/shard_map/ppermute | solution.py:98
  296.3 2.7 add_convert_fusion.7
  299.2 2.4 collective-permute-done.5.refs_0_
  301.6 2.4 add_convert_fusion.4
  304.0 1.5 collective-permute-start.6
  305.5 13.4 %collective-permute-done.4 = bf16[192,1536]{1,0:T(8,128)(2,1)} collective-permute-done((bf16[192,1536]{1,0:T(8,128)(2,1)}, bf16[192,1536]{1,0:T(8,128)(2,1)}, u32[]{:S(2)}, u32[]{:S(2)}) %collective-permute-start.4) | collective-permute-done | bytes 589856 | tf_op jit(solution)/shard_map/ppermute | solution.py:98
  318.9 1.8 add_convert_fusion.14.refs_0_
  320.6 2.3 collective-permute-start.8
  323.0 1.9 add_convert_fusion.11
  324.9 1.1 collective-permute-start.7
  326.0 8.4 %collective-permute-done.8.refs_0_ = bf16[96,1536]{1,0:T(8,128)(2,1)S(1)} collective-permute-done((bf16[96,1536]{1,0:T(8,128)(2,1)}, bf16[96,1536]{1,0:T(8,128)(2,1)S(1)}, u32[]{:S(2)}, u32[]{:S(2)}) %collective-permute-start.8) | collective-permute-done | bytes 294944 | tf_op jit(solution)/shard_map/ppermute | solution.py:98
  335.1 1.9 add_convert_fusion.12.refs_1_
  338.4 1.1 copy-done.3
  339.6 7.5 %collective-permute-done.9 = bf16[24,3200]{1,0:T(8,128)(2,1)S(1)} collective-permute-done((bf16[24,3200]{1,0:T(8,128)(2,1)}, bf16[24,3200]{1,0:T(8,128)(2,1)S(1)}, u32[]{:S(2)}, u32[]{:S(2)}) %collective-permute-start.9) | collective-permute-done | bytes 153632 | tf_op jit(solution)/shard_map/ppermute | solution.py:98
  347.8 7.4 %collective-permute-done.10 = bf16[24,3200]{1,0:T(8,128)(2,1)S(1)} collective-permute-done((bf16[24,3200]{1,0:T(8,128)(2,1)}, bf16[24,3200]{1,0:T(8,128)(2,1)S(1)}, u32[]{:S(2)}, u32[]{:S(2)}) %collective-permute-start.10) | collective-permute-done | bytes 153632 | tf_op jit(solution)/shard_map/ppermute | solution.py:98
  355.2 0.9 broadcast_select_fusion.5
  356.1 0.7 pad_maximum_fusion.2.refs_0_
  356.9 8.6 %collective-permute-done.11 = bf16[48,3200]{1,0:T(8,128)(2,1)S(1)} collective-permute-done((bf16[48,3200]{1,0:T(8,128)(2,1)}, bf16[48,3200]{1,0:T(8,128)(2,1)S(1)}, u32[]{:S(2)}, u32[]{:S(2)}) %collective-permute-start.11) | collective-permute-done | bytes 307232 | tf_op jit(solution)/shard_map/ppermute | solution.py:98
  365.5 1.0 broadcast_select_fusion.3
  366.5 0.9 pad_maximum_fusion.1.refs_0_
  367.4 4.7 %collective-permute-start.12 = (bf16[96,3200]{1,0:T(8,128)(2,1)}, bf16[96,3200]{1,0:T(8,128)(2,1)S(1)}, u32[]{:S(2)}, u32[]{:S(2)}) collective-permute-start(bf16[96,3200]{1,0:T(8,128)(2,1)} %tied.39.refs_0_), channel_id=1, source_target_pairs={{0,1},{1,0},{2,3},{3,2},{4,5},{5,4},{6,7},{7,6},{8,9},{9,8},{10,11... | collective-permute-start | bytes 1843208 | tf_op jit(solution)/shard_map/ppermute | solution.py:98
  372.1 2.7 copied.4
  374.8 2.7 copied.5
  377.5 8.9 %collective-permute-done.12 = bf16[96,3200]{1,0:T(8,128)(2,1)S(1)} collective-permute-done((bf16[96,3200]{1,0:T(8,128)(2,1)}, bf16[96,3200]{1,0:T(8,128)(2,1)S(1)}, u32[]{:S(2)}, u32[]{:S(2)}) %collective-permute-start.12) | collective-permute-done | bytes 614432 | tf_op jit(solution)/shard_map/ppermute | solution.py:98
  388.3 1.3 slice.125
  389.6 1.1 slice_reduce_fusion
  390.7 0.9 maximum_convert_fusion.1
  391.5 22.2 %all-gather.11.cloned.1.call-done = bf16[768,1536]{1,0:T(8,128)(2,1)} async-done(((bf16[96,1536]{1,0:T(8,128)(2,1)}), bf16[768,1536]{1,0:T(8,128)(2,1)}) %all-gather.11.cloned.1.call-update) | async-done | bytes 2359312 | tf_op jit(solution)/shard_map/all_gather | solution.py:921
  413.7 4.1 spread_gradients.1
  (123 shorter events, 12.9 us)
Async XLA Ops:
  7.2 65.3 %copy-start = (s32[8,1024]{1,0:T(8,128)S(1)}, s32[8,1024]{1,0:T(8,128)}, u32[]{:S(2)}) copy-start(s32[8,1024]{1,0:T(8,128)} %param.17) | copy-start | bytes 98308
  7.2 69.0 %all-gather.7.cloned.1.call-start = ((), (), s32[]{:S(2)}) async-start(), calls=%async_computation.7 | async-start | bytes 4792320 | tf_op jit(solution)/shard_map/all_gather | solution.py:829
  9.5 108.3 %all-gather.9.cloned.1.call-start = ((), (), s32[]{:S(2)}) async-start(), calls=%async_computation.8 | async-start | bytes 13271040 | tf_op jit(solution)/shard_map/all_gather | solution.py:830
  13.1 7.3 %copy-start.13 = (s32[8,2,12,3]{2,1,3,0:T(2,128)S(1)}, s32[8,2,12,3]{2,1,3,0:T(2,128)}, u32[]{:S(2)}) copy-start(s32[8,2,12,3]{2,1,3,0:T(2,128)} %param.18) | copy-start | bytes 6916
  13.1 44.3 %all-to-all-start = ((bf16[8,128,768]{2,1,0:T(8,128)(2,1)}), bf16[8,128,768]{2,1,0:T(8,128)(2,1)S(1)}, u32[]{:S(2)}, u32[]{:S(2)}) async-start(bf16[8,128,768]{2,1,0:T(8,128)(2,1)} %param.16), calls=%async_computation | async-start | bytes 3145728 | tf_op jit(solution)/shard_map/all_to_all | solution.py:26
  57.4 1.1 copy-start.2
  58.6 10.0 %all-to-all-start.1 = ((s32[8,1,72]{2,1,0:T(1,128)}), s32[8,1,72]{2,1,0:T(1,128)S(1)}, u32[]{:S(2)}, u32[]{:S(2)}) async-start(s32[8,1,72]{2,1,0:T(1,128)} %tied.20), calls=%async_computation.1 | async-start | bytes 8192 | tf_op jit(solution)/shard_map/all_to_all | solution.py:26
  68.6 39.9 %all-to-all-start.2 = ((bf16[8,128,768]{2,1,0:T(8,128)(2,1)}), bf16[8,128,768]{2,1,0:T(8,128)(2,1)S(1)}, u32[]{:S(2)}, u32[]{:S(2)}) async-start(bf16[8,128,768]{2,1,0:T(8,128)(2,1)} %copied.3), calls=%async_computation.2 | async-start | bytes 3145728 | tf_op jit(solution)/shard_map/all_to_all | solution.py:26
  72.2 168.3 %reduce-scatter.2.cloned.1.call-start = ((), (), s32[]{:S(2)}) async-start(), calls=%async_computation.6 | async-start | bytes 5898240 | tf_op jit(solution)/shard_map/reduce_scatter | solution.py:156
  108.5 9.4 %copy-start.7 = (bf16[8,128,768]{2,1,0:T(8,128)(2,1)}, bf16[8,128,768]{2,1,0:T(8,128)(2,1)S(1)}, u32[]{:S(2)}) copy-start(bf16[8,128,768]{2,1,0:T(8,128)(2,1)S(1)} %all-to-all-done.2) | copy-start | bytes 4718596
  176.1 6.3 %collective-permute-start = (bf16[1536,768]{1,0:T(8,128)(2,1)}, bf16[1536,768]{1,0:T(8,128)(2,1)}, u32[]{:S(2)}, u32[]{:S(2)}) collective-permute-start(bf16[1536,768]{1,0:T(8,128)(2,1)} %tied.21.refs_1_), channel_id=1, source_target_pairs={{0,8},{8,0},{16,24},{24,16},{1,9},{9,1},{17,25},{25,17},{2,10},{10... | collective-permute-start | bytes 7077896 | tf_op jit(solution)/shard_map/ppermute | solution.py:128
  176.4 67.4 %all-to-all-start.3 = ((bf16[8,128,768]{2,1,0:T(8,128)(2,1)}), bf16[8,128,768]{2,1,0:T(8,128)(2,1)S(1)}, u32[]{:S(2)}, u32[]{:S(2)}) async-start(bf16[8,128,768]{2,1,0:T(8,128)(2,1)} %bitcast.59), calls=%async_computation.3 | async-start | bytes 3145728 | tf_op jit(solution)/shard_map/all_to_all | solution.py:26
  186.4 51.5 %collective-permute-start.1 = (bf16[768,768]{1,0:T(8,128)(2,1)}, bf16[768,768]{1,0:T(8,128)(2,1)}, u32[]{:S(2)}, u32[]{:S(2)}) collective-permute-start(bf16[768,768]{1,0:T(8,128)(2,1)} %tied.23.refs_7_), channel_id=1, source_target_pairs={{0,16},{8,24},{16,0},{24,8},{1,17},{9,25},{17,1},{25,9},{2,18},{10... | collective-permute-start | bytes 3538952 | tf_op jit(solution)/shard_map/ppermute | solution.py:128
  188.3 48.8 %copy-start.14 = (f32[8,768]{1,0:T(8,128)S(1)}, f32[8,768]{1,0:T(8,128)}, u32[]{:S(2)}) copy-start(f32[8,768]{1,0:T(8,128)} %get-tuple-element.53) | copy-start | bytes 73732
  240.5 2.2 copy-start.11
  243.8 1.1 copy-start.4
  256.8 1.3 copy-start.5
  256.8 12.0 %collective-permute-start.3 = (bf16[384,3200]{1,0:T(8,128)(2,1)}, bf16[384,3200]{1,0:T(8,128)(2,1)}, u32[]{:S(2)}, u32[]{:S(2)}) collective-permute-start(bf16[384,3200]{1,0:T(8,128)(2,1)} %tied.26.refs_5_.refs_1_), channel_id=1, source_target_pairs={{0,8},{8,0},{16,24},{24,16},{1,9},{9,1},{17,25},{25,17},{2,10},{10... | collective-permute-start | bytes 7372808 | tf_op jit(solution)/shard_map/ppermute | solution.py:128
  258.1 38.2 %collective-permute-start.2 = (bf16[384,1536]{1,0:T(8,128)(2,1)S(1)}, bf16[384,1536]{1,0:T(8,128)(2,1)}, u32[]{:S(2)}, u32[]{:S(2)}) collective-permute-start(bf16[384,1536]{1,0:T(8,128)(2,1)S(1)} %copy-done.5), channel_id=1, source_target_pairs={{0,1},{1,0},{2,3},{3,2},{4,5},{5,4},{6,7},{7,6},{8,9},{9,8},{10,11... | collective-permute-start | bytes 3538952 | tf_op jit(solution)/shard_map/ppermute | solution.py:98
  273.2 28.4 %collective-permute-start.5 = (bf16[192,3200]{1,0:T(8,128)(2,1)}, bf16[192,3200]{1,0:T(8,128)(2,1)}, u32[]{:S(2)}, u32[]{:S(2)}) collective-permute-start(bf16[192,3200]{1,0:T(8,128)(2,1)} %tied.28.refs_1_), channel_id=1, source_target_pairs={{0,16},{8,24},{16,0},{24,8},{1,17},{9,25},{17,1},{25,9},{2,18},{10... | collective-permute-start | bytes 3686408 | tf_op jit(solution)/shard_map/ppermute | solution.py:128
  274.8 21.5 %copy-start.10 = (bf16[384,768]{1,0:T(8,128)(2,1)S(1)}, bf16[384,768]{1,0:T(8,128)(2,1)}, u32[]{:S(2)}) copy-start(bf16[384,768]{1,0:T(8,128)(2,1)} %get-tuple-element.75) | copy-start | bytes 1769476
  274.8 63.6 %all-to-all-start.4 = ((bf16[8,128,768]{2,1,0:T(8,128)(2,1)}), bf16[8,128,768]{2,1,0:T(8,128)(2,1)S(1)}, u32[]{:S(2)}, u32[]{:S(2)}) async-start(bf16[8,128,768]{2,1,0:T(8,128)(2,1)} %bitcast.50), calls=%async_computation.5 | async-start | bytes 3145728 | tf_op jit(solution)/shard_map/all_to_all | solution.py:26
  279.4 134.3 %all-gather.11.cloned.1.call-start = ((), (), s32[]{:S(2)}) async-start(), calls=%async_computation.9 | async-start | bytes 2654208 | tf_op jit(solution)/shard_map/all_gather | solution.py:921
  299.0 2.6 copy-start.8
  299.0 19.9 %collective-permute-start.4 = (bf16[192,1536]{1,0:T(8,128)(2,1)}, bf16[192,1536]{1,0:T(8,128)(2,1)}, u32[]{:S(2)}, u32[]{:S(2)}) collective-permute-start(bf16[192,1536]{1,0:T(8,128)(2,1)} %tied.29.refs_1_), channel_id=1, source_target_pairs={{0,2},{1,3},{2,0},{3,1},{4,6},{5,7},{6,4},{7,5},{8,10},{9,11},{10,... | collective-permute-start | bytes 1769480 | tf_op jit(solution)/shard_map/ppermute | solution.py:98
  304.0 14.9 %copy-start.9 = (bf16[192,1536]{1,0:T(8,128)(2,1)S(1)}, bf16[192,1536]{1,0:T(8,128)(2,1)}, u32[]{:S(2)}) copy-start(bf16[192,1536]{1,0:T(8,128)(2,1)} %get-tuple-element.72) | copy-start | bytes 1769476
  304.0 19.0 %collective-permute-start.6 = (bf16[96,3200]{1,0:T(8,128)(2,1)}, bf16[96,3200]{1,0:T(8,128)(2,1)}, u32[]{:S(2)}, u32[]{:S(2)}) collective-permute-start(bf16[96,3200]{1,0:T(8,128)(2,1)} %tied.31.refs_1_), channel_id=1, source_target_pairs={{0,1},{1,0},{2,3},{3,2},{4,5},{5,4},{6,7},{7,6},{8,9},{9,8},{10,11... | collective-permute-start | bytes 1843208 | tf_op jit(solution)/shard_map/ppermute | solution.py:98
  320.6 13.8 %collective-permute-start.8 = (bf16[96,1536]{1,0:T(8,128)(2,1)}, bf16[96,1536]{1,0:T(8,128)(2,1)S(1)}, u32[]{:S(2)}, u32[]{:S(2)}) collective-permute-start(bf16[96,1536]{1,0:T(8,128)(2,1)} %tied.32.refs_0_.refs_1_), channel_id=1, source_target_pairs={{0,4},{1,5},{2,6},{3,7},{4,0},{5,1},{6,2},{7,3},{8,12},{9,13},{10,... | collective-permute-start | bytes 884744 | tf_op jit(solution)/shard_map/ppermute | solution.py:98
  324.9 12.8 %collective-permute-start.7 = (bf16[48,3200]{1,0:T(8,128)(2,1)}, bf16[48,3200]{1,0:T(8,128)(2,1)S(1)}, u32[]{:S(2)}, u32[]{:S(2)}) collective-permute-start(bf16[48,3200]{1,0:T(8,128)(2,1)} %tied.34.refs_1_), channel_id=1, source_target_pairs={{0,2},{1,3},{2,0},{3,1},{4,6},{5,7},{6,4},{7,5},{8,10},{9,11},{10,... | collective-permute-start | bytes 921608 | tf_op jit(solution)/shard_map/ppermute | solution.py:98
  334.4 0.7 copy-start.12
  338.4 1.1 copy-start.3
  339.6 7.5 %collective-permute-start.9 = (bf16[24,3200]{1,0:T(8,128)(2,1)}, bf16[24,3200]{1,0:T(8,128)(2,1)S(1)}, u32[]{:S(2)}, u32[]{:S(2)}) collective-permute-start(bf16[24,3200]{1,0:T(8,128)(2,1)} %tied.36), channel_id=1, source_target_pairs={{0,4},{1,5},{2,6},{3,7},{4,0},{5,1},{6,2},{7,3},{8,12},{9,13},{10,... | collective-permute-start | bytes 460808 | tf_op jit(solution)/shard_map/ppermute | solution.py:98
  347.8 7.4 %collective-permute-start.10 = (bf16[24,3200]{1,0:T(8,128)(2,1)}, bf16[24,3200]{1,0:T(8,128)(2,1)S(1)}, u32[]{:S(2)}, u32[]{:S(2)}) collective-permute-start(bf16[24,3200]{1,0:T(8,128)(2,1)} %tied.37), channel_id=1, source_target_pairs={{0,4},{1,5},{2,6},{3,7},{4,0},{5,1},{6,2},{7,3},{8,12},{9,13},{10,... | collective-permute-start | bytes 460808 | tf_op jit(solution)/shard_map/ppermute | solution.py:98
  356.9 8.6 %collective-permute-start.11 = (bf16[48,3200]{1,0:T(8,128)(2,1)}, bf16[48,3200]{1,0:T(8,128)(2,1)S(1)}, u32[]{:S(2)}, u32[]{:S(2)}) collective-permute-start(bf16[48,3200]{1,0:T(8,128)(2,1)} %tied.38), channel_id=1, source_target_pairs={{0,2},{1,3},{2,0},{3,1},{4,6},{5,7},{6,4},{7,5},{8,10},{9,11},{10,... | collective-permute-start | bytes 921608 | tf_op jit(solution)/shard_map/ppermute | solution.py:98
  367.4 19.0 %collective-permute-start.12 = (bf16[96,3200]{1,0:T(8,128)(2,1)}, bf16[96,3200]{1,0:T(8,128)(2,1)S(1)}, u32[]{:S(2)}, u32[]{:S(2)}) collective-permute-start(bf16[96,3200]{1,0:T(8,128)(2,1)} %tied.39.refs_0_), channel_id=1, source_target_pairs={{0,1},{1,0},{2,3},{3,2},{4,5},{5,4},{6,7},{7,6},{8,9},{9,8},{10,11... | collective-permute-start | bytes 1843208 | tf_op jit(solution)/shard_map/ppermute | solution.py:98
  374.8 11.6 %copy-start.6 = (bf16[96,3200]{1,0:T(8,128)(2,1)S(1)}, bf16[96,3200]{1,0:T(8,128)(2,1)}, u32[]{:S(2)}) copy-start(bf16[96,3200]{1,0:T(8,128)(2,1)} %tied.39.refs_0_) | copy-start | bytes 1843204
  390.7 27.2 %copy-start.1 = (s32[8,1024]{1,0:T(8,128)S(1)}, s32[8,1024]{1,0:T(8,128)}, u32[]{:S(2)}) copy-start(s32[8,1024]{1,0:T(8,128)} %param.17) | copy-start | bytes 98308
Sparse Core Ops, SparseCore 0:
  10.2 35.1 all-gather.6
  46.9 70.9 all-gather.8
  165.6 70.6 reduce-scatter.1
  357.0 56.6 all-gather.10

commit v2 on v1

--- a/solution.py
+++ b/solution.py
@@ -231,7 +231,19 @@
 
 
 def forward_kernel(
-    q_ref, k_ref, v_ref, key_feat_ref, query_feat_ref, table_ref, out_ref, keys, vals, *, half, tile
+    q_ref,
+    k_ref,
+    v_ref,
+    key_feat_ref,
+    query_feat_ref,
+    table_ref,
+    out_ref,
+    log_ref,
+    keys,
+    vals,
+    *,
+    half,
+    tile,
 ):
     tokens = q_ref.shape[0]
     fill_keys(k_ref, key_feat_ref, table_ref, keys)
@@ -252,12 +264,15 @@
             )
             for side in range(2)
         ]
-        outs = []
+        outs, logs = [], []
         for score in scores:
-            weights = jnp.exp(score - jnp.max(score, axis=1, keepdims=True)).astype(bf16)
+            top = jnp.max(score, axis=1, keepdims=True)
+            weights = jnp.exp(score - top).astype(bf16)
             mixed = dot(weights, vals[...])
             outs.append(mixed[:, :lanes_n] / mixed[:, lanes_n:])
+            logs.append(top + jnp.log(mixed[:, lanes_n:]))
         out_ref[rows, :] = jnp.where(side_of == 0, outs[0], outs[1]).astype(bf16)
+        log_ref[rows, :] = jnp.where(side_of == 0, logs[0], logs[1])
 
 
 def backward_kernel(
@@ -265,6 +280,8 @@
     k_ref,
     v_ref,
     grad_ref,
+    out_ref,
+    log_ref,
     key_feat_ref,
     query_feat_ref,
     table_ref,
@@ -295,14 +312,14 @@
         queries = [jnp.where(side_of == side, q_pair, bf16(0)) for side in range(2)]
         grads = [jnp.where(side_of == side, grad_pair, bf16(0)) for side in range(2)]
         probs, dscores = [], []
+        product = grad_pair.astype(f32) * out_ref[rows, :].astype(f32)
         for side in range(2):
             wide = jnp.concatenate([queries[side], feat], axis=1)
             scores = dot(wide, keys[side], rows_by_rows)
             dprobs = dot(grads[side], v_ref[...], rows_by_rows)
-            raw = jnp.exp(scores - jnp.max(scores, axis=1, keepdims=True))
-            prob = raw * (1.0 / jnp.sum(raw, axis=1, keepdims=True))
-            both = prob * dprobs
-            dscore = both - prob * jnp.sum(both, axis=1, keepdims=True)
+            prob = jnp.exp(scores - log_ref[rows, side * half : side * half + 1])
+            inner = jnp.sum(jnp.where(side_of == side, product, 0.0), axis=1, keepdims=True)
+            dscore = prob * (dprobs - inner)
             probs.append(prob.astype(bf16))
             dscores.append(dscore.astype(bf16))
         dv_sum[...] += dot(
@@ -350,9 +367,10 @@
         + [whole, whole]
         + [pl.BlockSpec((2,) + table.shape[1:], lambda p: (p + first, 0, 0))]
         + [pl.BlockSpec(memory_space=pl.ANY)] * len(after),
-        out_specs=[pair_out] * outs + [pl.BlockSpec((8, lanes_n), lambda p: (0, p))] * (outs > 1),
+        out_specs=[pair_out] * outs
+        + [pl.BlockSpec((8, lanes_n), lambda p: (0, p)) if outs > 1 else pair_out],
         out_shape=[shape] * outs
-        + [jax.ShapeDtypeStruct((8, count * lanes_n), f32)] * (outs > 1),
+        + [jax.ShapeDtypeStruct((8 if outs > 1 else tokens, count * lanes_n), f32)],
         scratch_shapes=scratch,
         compiler_params=pltpu.CompilerParams(vmem_limit_bytes=vmem_cap),
         cost_estimate=pl.CostEstimate(flops=0, bytes_accessed=tokens, transcendentals=0),
@@ -868,7 +886,9 @@
     queries, keys, values = project(x, first, bias_qv)
     grad_result = swap_pieces(copied(cotangent, x), "ctx", team).reshape(tokens, width)
     heads = tuple(to_heads(part) for part in (queries, keys, values))
-    attended = attend(forward_kernel, heads, features, 1, head_size, "attend_forward")[0]
+    attended = attend(forward_kernel, heads, features, 1, head_size, "attend_forward")
+    attended, log_total = attended
+    kept = (attended, log_total)
     attended = to_tokens(attended)
     parts = token_parts(attended, x, grad_result, others, vecs, bias_up)
     result, hidden_low, active, grad_mlp, grad_upper, grad_pre, grad_branch, grad_att, sums, sums_up = parts
@@ -881,7 +901,7 @@
     layer_out = back_to_runs(tied(result, sent))
     up.end()
     sent = up.begin(sent)
-    back_heads = heads + (to_heads(grad_att),)
+    back_heads = heads + (to_heads(grad_att),) + kept
     pair_count = back_heads[0].shape[1] // lanes_n
     back = attend(backward_kernel, back_heads, features, 3, head_size, "attend_backward", (sent,))
     if team > 1:

time: 432 us -> 425 us (0.984); the launches traced: 425 us -> 423 us
  waiting for transfers between devices: 146 us -> 153 us
  Pallas kernels: 173 us -> 167 us
    ppermute x4, waiting for transfers between devices: 2.44 us -> 8.27 us  [begin(): lax.ppermute(sent, 'dp', [(i, i ^ self.stride) for i in range(size)])]
    pallas_call x2, Pallas kernels: 68.1 us -> 62.8 us  [attend(): pl.pallas_call(run, grid=(count,), in_specs=[pair] * len(arrays) + [whole...]
  transfers between devices with their start and end apart: 22 -> 22, of which waited for: 13 -> 14; matrix products, arithmetic and copies ran while one was open for 11% -> 11% of each run, Pallas kernels for 25% -> 24%
where the time goes in v2:
time: 425 us; the launch traced here: 423 us
  Pallas kernels  167 us (39%)
  waiting for transfers between devices  153 us (36%)
  starting transfers between devices  36.7 us (9%)
  other arithmetic  34.4 us (8%)
  local copies, waits for them, and re-layouts  18.1 us (4%)
  between operations  14.1 us (3%)
    ppermute x9, waiting for transfers between devices, begin(): lax.ppermute(sent, self.axis, [(i, i ^ stride) for i in range(size)])  74.4 us
    pallas_call x2, Pallas kernels, attend(): pl.pallas_call(run, grid=(count,), in_specs=[pair] * len(arrays) + [whole...  62.8 us
    all_to_all x5, waiting for transfers between devices, swap_pieces(): lax.all_to_all(pieces, axis, 0, 0, axis_index_groups=groups, tiled=True)  39.9 us
    pallas_call x1, Pallas kernels, token_parts(): pl.pallas_call(token_kernel, grid=(tokens // tile,), in_specs=[row(width)...  38.4 us
    all_to_all x5, starting transfers between devices, swap_pieces(): lax.all_to_all(pieces, axis, 0, 0, axis_index_groups=groups, tiled=True)  25 us
    convert_element_type x10, other arithmetic, added(): return total.astype(bf16)  23 us
    all_gather x1, waiting for transfers between devices, body(): pieces = lax.all_gather(pieces, 'ctx', axis=0)  21.9 us
    pallas_call x1, Pallas kernels, weight_grads(): pl.pallas_call(functools.partial(grads_kernel, groups=places, held=held,...  11.7 us
  transfers between devices with their start and end apart: 22, of which 14 were waited for; matrix products, arithmetic and copies ran while one was open for 11% of the time, Pallas kernels for 24%

profile of v2, /device:TPU:0, one launch (start us, length us, event | category | flops | bytes accessed | tf_op | source)
XLA Modules:
  0.0 423.5 jit_solution(7119153744290391285)
XLA Ops:
  7.2 2.3 pack_weights.1
  9.6 3.5 join_weights.1
  13.1 7.3 %all-to-all-start = ((bf16[8,128,768]{2,1,0:T(8,128)(2,1)}), bf16[8,128,768]{2,1,0:T(8,128)(2,1)S(1)}, u32[]{:S(2)}, u32[]{:S(2)}) async-start(bf16[8,128,768]{2,1,0:T(8,128)(2,1)} %param.16), calls=%async_computation | async-start | bytes 3145728 | tf_op jit(solution)/shard_map/all_to_all | solution.py:26
  21.2 36.2 %all-to-all-done = bf16[8,128,768]{2,1,0:T(8,128)(2,1)S(1)} async-done(((bf16[8,128,768]{2,1,0:T(8,128)(2,1)}), bf16[8,128,768]{2,1,0:T(8,128)(2,1)S(1)}, u32[]{:S(2)}, u32[]{:S(2)}) %all-to-all-start) | async-done | bytes 1572896 | tf_op jit(solution)/shard_map/all_to_all | solution.py:26
  57.4 1.1 copy-done.2
  58.5 3.6 all-to-all-start.1
  62.2 2.7 copied.3
  64.8 3.7 all-to-all-done.1
  68.6 3.6 all-to-all-start.2
  72.6 1.1 select_convert_fusion
  75.4 0.8 maximum_maximum_fusion.1.refs_5_.refs_8_
  76.2 0.7 slice.116
  76.9 0.8 slice.120
  78.3 7.6 %project.1 = (bf16[1024,768]{1,0:T(8,128)(2,1)}, bf16[1024,768]{1,0:T(8,128)(2,1)}, bf16[1024,768]{1,0:T(8,128)(2,1)}) custom-call(bf16[1024,768]{1,0:T(8,128)(2,1)} %bitcast.47, bf16[4,208,2304]{2,1,0:T(8,128)(2,1)} %bitcast.53, f32[1,1536]{1,0:T(1,128)} %convert.2.bias_ref), custom_call_target="tpu_custom_call" | custom-call | bytes 1024 | tf_op jit(solution)/shard_map/project/pallas_call | solution.py:440
  87.5 20.9 %attend_forward.1 = (bf16[1024,768]{1,0:T(8,128)(2,1)}, f32[1024,768]{1,0:T(8,128)}) custom-call(bf16[1024,768]{1,0:T(8,128)(2,1)} %get-tuple-element.39.refs_0_, bf16[1024,768]{1,0:T(8,128)(2,1)} %get-tuple-element.40.refs_1_, bf16[1024,768]{1,0:T(8,128)(2,1)} %get-tuple-element.41.refs_2_, bf16[1024,128]{1,0:T(8,128)(2,1)} %get-tuple-element.95.refs_3_.refs_6_, ...), custom_call_target="tpu_custom_call" | custom-call | bytes 1024 | tf_op jit(solution)/shard_map/attend_forward/pallas_call | solution.py:363
  109.0 8.8 %all-gather.9.cloned.1.call-done = bf16[768,6912]{1,0:T(8,128)(2,1)} async-done(((bf16[192,6912]{1,0:T(8,128)(2,1)}), bf16[768,6912]{1,0:T(8,128)(2,1)}) %all-gather.9.cloned.1.call-update) | async-done | bytes 10616848 | tf_op jit(solution)/shard_map/all_gather | solution.py:848
  117.9 38.4 %token_parts.1 = (bf16[1024,768]{1,0:T(8,128)(2,1)}, bf16[1024,768]{1,0:T(8,128)(2,1)}, bf16[1024,3072]{1,0:T(8,128)(2,1)}, bf16[1024,768]{1,0:T(8,128)(2,1)}, b...) custom-call(bf16[1024,768]{1,0:T(8,128)(2,1)} %get-tuple-element.42., ...), custom_call_target="tpu_custom_call" | custom-call | bytes 1024 | tf_op jit(solution)/shard_map/token_parts/pallas_call | solution.py:768
  156.3 9.2 %matrix_grad.1.refs_0_ = bf16[3072,768]{1,0:T(8,128)(2,1)} custom-call(bf16[1024,3072]{1,0:T(8,128)(2,1)} %get-tuple-element.46.left_ref, bf16[1024,768]{1,0:T(8,128)(2,1)} %get-tuple-element.47.right_ref), custom_call_target="tpu_custom_call" | custom-call | bytes 768 | tf_op jit(solution)/shard_map/matrix_grad/pallas_call | solution.py:547
  165.4 10.6 %wide_grad.1 = (bf16[1536,768]{1,0:T(8,128)(2,1)}, bf16[1536,768]{1,0:T(8,128)(2,1)}) custom-call(s32[1]{0:T(128)} %bitcast.9.place_ref, bf16[1024,768]{1,0:T(8,128)(2,1)} %get-tuple-element.44.left_ref, bf16[1024,3072]{1,0:T(8,128)(2,1)} %get-tuple-element.45.right_ref, bf16[3072,768]{1,0:T(8,128)(2,1)} %matrix_grad.1.refs_0_), custom_call_target="tpu_custom_call" | custom-call | bytes 768 | tf_op jit(solution)/shard_map/wide_grad/pallas_call | solution.py:517
  176.4 5.7 %all-to-all-start.3 = ((bf16[8,128,768]{2,1,0:T(8,128)(2,1)}), bf16[8,128,768]{2,1,0:T(8,128)(2,1)S(1)}, u32[]{:S(2)}, u32[]{:S(2)}) async-start(bf16[8,128,768]{2,1,0:T(8,128)(2,1)} %bitcast.59), calls=%async_computation.3 | async-start | bytes 3145728 | tf_op jit(solution)/shard_map/all_to_all | solution.py:26
  182.2 3.9 add_convert_fusion.3
  186.1 0.7 collective-permute-start.1
  186.9 0.9 slice_reduce_fusion.6
  188.0 41.9 %attend_backward.1 = (bf16[1024,768]{1,0:T(8,128)(2,1)}, bf16[1024,768]{1,0:T(8,128)(2,1)}, bf16[1024,768]{1,0:T(8,128)(2,1)}, f32[8,768]{1,0:T(8,128)}) custom-call(bf16[1024,768]{1,0:T(8,128)(2,1)} %get-tuple-element.39.refs_0_, bf16[1024,768]{1,0:T(8,128)(2,1)} %get-tuple-element.40.refs_1_, bf16[1024,768]{1,0:T(8,128)(2,1)} %get-tuple-element.41.refs_2_, ...), custom_call_target="tpu_custom_call" | custom-call | bytes 1024 | tf_op jit(solution)/shard_map/attend_backward/pallas_call | solution.py:363
  230.9 0.9 maximum_maximum_fusion.refs_6_
  231.7 5.6 %collective-permute-done.1.refs_0_ = bf16[768,768]{1,0:T(8,128)(2,1)} collective-permute-done((bf16[768,768]{1,0:T(8,128)(2,1)}, bf16[768,768]{1,0:T(8,128)(2,1)}, u32[]{:S(2)}, u32[]{:S(2)}) %collective-permute-start.1) | collective-permute-done | bytes 1179680 | tf_op jit(solution)/shard_map/ppermute | solution.py:128
  237.3 2.5 add_convert_fusion.8
  239.9 2.2 constant_dynamic-slice_fusion
  242.1 1.1 pad_maximum_fusion.refs_0_
  243.2 1.1 copy-done.4
  244.3 11.7 %weight_grads.1 = (bf16[384,3200]{1,0:T(8,128)(2,1)}, bf16[384,3200]{1,0:T(8,128)(2,1)}) custom-call(s32[1]{0:T(128)} %bitcast.9.place_ref, bf16[1024,768]{1,0:T(8,128)(2,1)} %get-tuple-element.42.attended_ref.refs_4_.refs_0_, bf16[1024,768]{1,0:T(8,128)(2,1)} %get-tuple-element.53.refs_1_, bf16[1024,768]{1,0:T(8,128)(2,1)} %bitcast.49, ...), custom_call_target="tpu_custom_call" | custom-call | bytes 3200 | tf_op jit(solution)/shard_map/weight_grads/pallas_call | solution.py:493
  256.0 1.3 copy-done.5
  257.3 1.5 collective-permute-start.2
  258.8 8.7 %input_gradient.1.refs_1_.refs_0_ = bf16[1024,768]{1,0:T(8,128)(2,1)} custom-call(bf16[4,208,2304]{2,1,0:T(8,128)(2,1)} %bitcast.55, f32[1024,768]{1,0:T(8,128)} %get-tuple-element.61.refs_1_, bf16[1024,768]{1,0:T(8,128)(2,1)} %get-tuple-element.52.refs_1_.refs_3_.refs_2_, bf16[1024,768]{1,0:T(8,128)(2,1)} %get-tuple-element.54.refs_4_.refs_3_, ...), custom_call_target="tpu_custom_call" | custom-call | bytes 1024 | tf_op jit(solution)/shard_map/input_gradient/pallas_call | solution.py:610
  267.5 4.4 %add_convert_fusion = (bf16[192,3200]{1,0:T(8,128)(2,1)}, bf16[192,3200]{1,0:T(8,128)(2,1)}) fusion(bf16[384,3200]{1,0:T(8,128)(2,1)} %tied.27, bf16[384,3200]{1,0:T(8,128)(2,1)} %get-tuple-element.59), kind=kLoop, calls=%fused_computation | loop fusion | flops 4915200 | bytes 7372800 | tf_op jit(solution)/shard_map/convert_element_type | solution.py:61
  272.5 4.7 %all-to-all-start.4 = ((bf16[8,128,768]{2,1,0:T(8,128)(2,1)}), bf16[8,128,768]{2,1,0:T(8,128)(2,1)S(1)}, u32[]{:S(2)}, u32[]{:S(2)}) async-start(bf16[8,128,768]{2,1,0:T(8,128)(2,1)} %bitcast.50), calls=%async_computation.5 | async-start | bytes 3145728 | tf_op jit(solution)/shard_map/all_to_all | solution.py:26
  277.3 17.7 %collective-permute-done.2 = bf16[384,1536]{1,0:T(8,128)(2,1)} collective-permute-done((bf16[384,1536]{1,0:T(8,128)(2,1)S(1)}, bf16[384,1536]{1,0:T(8,128)(2,1)}, u32[]{:S(2)}, u32[]{:S(2)}) %collective-permute-start.2) | collective-permute-done | bytes 1179680 | tf_op jit(solution)/shard_map/ppermute | solution.py:98
  295.0 2.7 add_convert_fusion.7
  297.9 2.6 collective-permute-done.5.refs_0_
  300.5 2.4 add_convert_fusion.4
  302.9 1.2 collective-permute-start.6
  304.1 13.9 %collective-permute-done.4 = bf16[192,1536]{1,0:T(8,128)(2,1)} collective-permute-done((bf16[192,1536]{1,0:T(8,128)(2,1)}, bf16[192,1536]{1,0:T(8,128)(2,1)}, u32[]{:S(2)}, u32[]{:S(2)}) %collective-permute-start.4) | collective-permute-done | bytes 589856 | tf_op jit(solution)/shard_map/ppermute | solution.py:98
  318.0 1.7 add_convert_fusion.14.refs_0_
  319.8 1.2 collective-permute-start.8
  321.0 1.9 add_convert_fusion.11
  323.0 2.2 collective-permute-start.7
  325.2 7.8 %collective-permute-done.8.refs_0_ = bf16[96,1536]{1,0:T(8,128)(2,1)S(1)} collective-permute-done((bf16[96,1536]{1,0:T(8,128)(2,1)}, bf16[96,1536]{1,0:T(8,128)(2,1)S(1)}, u32[]{:S(2)}, u32[]{:S(2)}) %collective-permute-start.8) | collective-permute-done | bytes 294944 | tf_op jit(solution)/shard_map/ppermute | solution.py:98
  333.8 1.9 add_convert_fusion.12.refs_1_
  337.1 1.1 copy-done.3
  338.4 8.3 %collective-permute-done.9 = bf16[24,3200]{1,0:T(8,128)(2,1)S(1)} collective-permute-done((bf16[24,3200]{1,0:T(8,128)(2,1)}, bf16[24,3200]{1,0:T(8,128)(2,1)S(1)}, u32[]{:S(2)}, u32[]{:S(2)}) %collective-permute-start.9) | collective-permute-done | bytes 153632 | tf_op jit(solution)/shard_map/ppermute | solution.py:98
  347.5 8.0 %collective-permute-done.10 = bf16[24,3200]{1,0:T(8,128)(2,1)S(1)} collective-permute-done((bf16[24,3200]{1,0:T(8,128)(2,1)}, bf16[24,3200]{1,0:T(8,128)(2,1)S(1)}, u32[]{:S(2)}, u32[]{:S(2)}) %collective-permute-start.10) | collective-permute-done | bytes 153632 | tf_op jit(solution)/shard_map/ppermute | solution.py:98
  355.5 0.9 broadcast_select_fusion.5
  357.2 9.4 %collective-permute-done.11 = bf16[48,3200]{1,0:T(8,128)(2,1)S(1)} collective-permute-done((bf16[48,3200]{1,0:T(8,128)(2,1)}, bf16[48,3200]{1,0:T(8,128)(2,1)S(1)}, u32[]{:S(2)}, u32[]{:S(2)}) %collective-permute-start.11) | collective-permute-done | bytes 307232 | tf_op jit(solution)/shard_map/ppermute | solution.py:98
  366.6 1.0 broadcast_select_fusion.3
  367.6 0.9 pad_maximum_fusion.1.refs_0_
  368.5 3.4 collective-permute-start.12
  371.9 2.7 copied.4
  374.6 2.7 copied.5
  377.3 8.5 %collective-permute-done.12 = bf16[96,3200]{1,0:T(8,128)(2,1)S(1)} collective-permute-done((bf16[96,3200]{1,0:T(8,128)(2,1)}, bf16[96,3200]{1,0:T(8,128)(2,1)S(1)}, u32[]{:S(2)}, u32[]{:S(2)}) %collective-permute-start.12) | collective-permute-done | bytes 614432 | tf_op jit(solution)/shard_map/ppermute | solution.py:98
  387.7 1.3 slice.125
  389.0 1.1 slice_reduce_fusion
  390.1 0.9 maximum_convert_fusion.1
  390.9 21.9 %all-gather.11.cloned.1.call-done = bf16[768,1536]{1,0:T(8,128)(2,1)} async-done(((bf16[96,1536]{1,0:T(8,128)(2,1)}), bf16[768,1536]{1,0:T(8,128)(2,1)}) %all-gather.11.cloned.1.call-update) | async-done | bytes 2359312 | tf_op jit(solution)/shard_map/all_gather | solution.py:941
  412.8 4.1 spread_gradients.1
  (123 shorter events, 13.9 us)
Async XLA Ops:
  7.2 65.3 %copy-start = (s32[8,1024]{1,0:T(8,128)S(1)}, s32[8,1024]{1,0:T(8,128)}, u32[]{:S(2)}) copy-start(s32[8,1024]{1,0:T(8,128)} %param.17) | copy-start | bytes 98308
  7.2 69.0 %all-gather.7.cloned.1.call-start = ((), (), s32[]{:S(2)}) async-start(), calls=%async_computation.7 | async-start | bytes 4792320 | tf_op jit(solution)/shard_map/all_gather | solution.py:847
  9.5 108.3 %all-gather.9.cloned.1.call-start = ((), (), s32[]{:S(2)}) async-start(), calls=%async_computation.8 | async-start | bytes 13271040 | tf_op jit(solution)/shard_map/all_gather | solution.py:848
  13.1 7.3 %copy-start.13 = (s32[8,2,12,3]{2,1,3,0:T(2,128)S(1)}, s32[8,2,12,3]{2,1,3,0:T(2,128)}, u32[]{:S(2)}) copy-start(s32[8,2,12,3]{2,1,3,0:T(2,128)} %param.18) | copy-start | bytes 6916
  13.1 44.3 %all-to-all-start = ((bf16[8,128,768]{2,1,0:T(8,128)(2,1)}), bf16[8,128,768]{2,1,0:T(8,128)(2,1)S(1)}, u32[]{:S(2)}, u32[]{:S(2)}) async-start(bf16[8,128,768]{2,1,0:T(8,128)(2,1)} %param.16), calls=%async_computation | async-start | bytes 3145728 | tf_op jit(solution)/shard_map/all_to_all | solution.py:26
  57.4 1.1 copy-start.2
  58.5 10.0 %all-to-all-start.1 = ((s32[8,1,72]{2,1,0:T(1,128)}), s32[8,1,72]{2,1,0:T(1,128)S(1)}, u32[]{:S(2)}, u32[]{:S(2)}) async-start(s32[8,1,72]{2,1,0:T(1,128)} %tied.20), calls=%async_computation.1 | async-start | bytes 8192 | tf_op jit(solution)/shard_map/all_to_all | solution.py:26
  68.6 40.5 %all-to-all-start.2 = ((bf16[8,128,768]{2,1,0:T(8,128)(2,1)}), bf16[8,128,768]{2,1,0:T(8,128)(2,1)S(1)}, u32[]{:S(2)}, u32[]{:S(2)}) async-start(bf16[8,128,768]{2,1,0:T(8,128)(2,1)} %copied.3), calls=%async_computation.2 | async-start | bytes 3145728 | tf_op jit(solution)/shard_map/all_to_all | solution.py:26
  72.2 167.7 %reduce-scatter.2.cloned.1.call-start = ((), (), s32[]{:S(2)}) async-start(), calls=%async_computation.6 | async-start | bytes 5898240 | tf_op jit(solution)/shard_map/reduce_scatter | solution.py:156
  109.0 8.8 %copy-start.7 = (bf16[8,128,768]{2,1,0:T(8,128)(2,1)}, bf16[8,128,768]{2,1,0:T(8,128)(2,1)S(1)}, u32[]{:S(2)}) copy-start(bf16[8,128,768]{2,1,0:T(8,128)(2,1)S(1)} %all-to-all-done.2) | copy-start | bytes 4718596
  176.1 6.1 %collective-permute-start = (bf16[1536,768]{1,0:T(8,128)(2,1)}, bf16[1536,768]{1,0:T(8,128)(2,1)}, u32[]{:S(2)}, u32[]{:S(2)}) collective-permute-start(bf16[1536,768]{1,0:T(8,128)(2,1)} %tied.21.refs_1_), channel_id=1, source_target_pairs={{0,8},{8,0},{16,24},{24,16},{1,9},{9,1},{17,25},{25,17},{2,10},{10... | collective-permute-start | bytes 7077896 | tf_op jit(solution)/shard_map/ppermute | solution.py:128
  176.4 66.8 %all-to-all-start.3 = ((bf16[8,128,768]{2,1,0:T(8,128)(2,1)}), bf16[8,128,768]{2,1,0:T(8,128)(2,1)S(1)}, u32[]{:S(2)}, u32[]{:S(2)}) async-start(bf16[8,128,768]{2,1,0:T(8,128)(2,1)} %bitcast.59), calls=%async_computation.3 | async-start | bytes 3145728 | tf_op jit(solution)/shard_map/all_to_all | solution.py:26
  186.1 51.3 %collective-permute-start.1 = (bf16[768,768]{1,0:T(8,128)(2,1)}, bf16[768,768]{1,0:T(8,128)(2,1)}, u32[]{:S(2)}, u32[]{:S(2)}) collective-permute-start(bf16[768,768]{1,0:T(8,128)(2,1)} %tied.23.refs_9_), channel_id=1, source_target_pairs={{0,16},{8,24},{16,0},{24,8},{1,17},{9,25},{17,1},{25,9},{2,18},{10... | collective-permute-start | bytes 3538952 | tf_op jit(solution)/shard_map/ppermute | solution.py:128
  188.0 42.8 %copy-start.14 = (f32[8,768]{1,0:T(8,128)S(1)}, f32[8,768]{1,0:T(8,128)}, u32[]{:S(2)}) copy-start(f32[8,768]{1,0:T(8,128)} %get-tuple-element.57) | copy-start | bytes 73732
  239.9 2.2 copy-start.11
  243.2 1.1 copy-start.4
  256.0 1.3 copy-start.5
  256.0 11.5 %collective-permute-start.3 = (bf16[384,3200]{1,0:T(8,128)(2,1)}, bf16[384,3200]{1,0:T(8,128)(2,1)}, u32[]{:S(2)}, u32[]{:S(2)}) collective-permute-start(bf16[384,3200]{1,0:T(8,128)(2,1)} %tied.26.refs_5_.refs_1_), channel_id=1, source_target_pairs={{0,8},{8,0},{16,24},{24,16},{1,9},{9,1},{17,25},{25,17},{2,10},{10... | collective-permute-start | bytes 7372808 | tf_op jit(solution)/shard_map/ppermute | solution.py:128
  257.3 37.7 %collective-permute-start.2 = (bf16[384,1536]{1,0:T(8,128)(2,1)S(1)}, bf16[384,1536]{1,0:T(8,128)(2,1)}, u32[]{:S(2)}, u32[]{:S(2)}) collective-permute-start(bf16[384,1536]{1,0:T(8,128)(2,1)S(1)} %copy-done.5), channel_id=1, source_target_pairs={{0,1},{1,0},{2,3},{3,2},{4,5},{5,4},{6,7},{7,6},{8,9},{9,8},{10,11... | collective-permute-start | bytes 3538952 | tf_op jit(solution)/shard_map/ppermute | solution.py:98
  271.9 28.6 %collective-permute-start.5 = (bf16[192,3200]{1,0:T(8,128)(2,1)}, bf16[192,3200]{1,0:T(8,128)(2,1)}, u32[]{:S(2)}, u32[]{:S(2)}) collective-permute-start(bf16[192,3200]{1,0:T(8,128)(2,1)} %tied.28.refs_1_), channel_id=1, source_target_pairs={{0,16},{8,24},{16,0},{24,8},{1,17},{9,25},{17,1},{25,9},{2,18},{10... | collective-permute-start | bytes 3686408 | tf_op jit(solution)/shard_map/ppermute | solution.py:128
  272.5 22.5 %copy-start.10 = (bf16[384,768]{1,0:T(8,128)(2,1)S(1)}, bf16[384,768]{1,0:T(8,128)(2,1)}, u32[]{:S(2)}) copy-start(bf16[384,768]{1,0:T(8,128)(2,1)} %get-tuple-element.79) | copy-start | bytes 1769476
  272.5 64.6 %all-to-all-start.4 = ((bf16[8,128,768]{2,1,0:T(8,128)(2,1)}), bf16[8,128,768]{2,1,0:T(8,128)(2,1)S(1)}, u32[]{:S(2)}, u32[]{:S(2)}) async-start(bf16[8,128,768]{2,1,0:T(8,128)(2,1)} %bitcast.50), calls=%async_computation.5 | async-start | bytes 3145728 | tf_op jit(solution)/shard_map/all_to_all | solution.py:26
  277.2 135.6 %all-gather.11.cloned.1.call-start = ((), (), s32[]{:S(2)}) async-start(), calls=%async_computation.9 | async-start | bytes 2654208 | tf_op jit(solution)/shard_map/all_gather | solution.py:941
  297.7 2.8 copy-start.8
  297.7 20.3 %collective-permute-start.4 = (bf16[192,1536]{1,0:T(8,128)(2,1)}, bf16[192,1536]{1,0:T(8,128)(2,1)}, u32[]{:S(2)}, u32[]{:S(2)}) collective-permute-start(bf16[192,1536]{1,0:T(8,128)(2,1)} %tied.29.refs_1_), channel_id=1, source_target_pairs={{0,2},{1,3},{2,0},{3,1},{4,6},{5,7},{6,4},{7,5},{8,10},{9,11},{10,... | collective-permute-start | bytes 1769480 | tf_op jit(solution)/shard_map/ppermute | solution.py:98
  302.9 15.1 %copy-start.9 = (bf16[192,1536]{1,0:T(8,128)(2,1)S(1)}, bf16[192,1536]{1,0:T(8,128)(2,1)}, u32[]{:S(2)}) copy-start(bf16[192,1536]{1,0:T(8,128)(2,1)} %get-tuple-element.76) | copy-start | bytes 1769476
  302.9 18.1 %collective-permute-start.6 = (bf16[96,3200]{1,0:T(8,128)(2,1)}, bf16[96,3200]{1,0:T(8,128)(2,1)}, u32[]{:S(2)}, u32[]{:S(2)}) collective-permute-start(bf16[96,3200]{1,0:T(8,128)(2,1)} %tied.31.refs_1_), channel_id=1, source_target_pairs={{0,1},{1,0},{2,3},{3,2},{4,5},{5,4},{6,7},{7,6},{8,9},{9,8},{10,11... | collective-permute-start | bytes 1843208 | tf_op jit(solution)/shard_map/ppermute | solution.py:98
  319.8 13.2 %collective-permute-start.8 = (bf16[96,1536]{1,0:T(8,128)(2,1)}, bf16[96,1536]{1,0:T(8,128)(2,1)S(1)}, u32[]{:S(2)}, u32[]{:S(2)}) collective-permute-start(bf16[96,1536]{1,0:T(8,128)(2,1)} %tied.32.refs_0_.refs_1_), channel_id=1, source_target_pairs={{0,4},{1,5},{2,6},{3,7},{4,0},{5,1},{6,2},{7,3},{8,12},{9,13},{10,... | collective-permute-start | bytes 884744 | tf_op jit(solution)/shard_map/ppermute | solution.py:98
  323.0 13.4 %collective-permute-start.7 = (bf16[48,3200]{1,0:T(8,128)(2,1)}, bf16[48,3200]{1,0:T(8,128)(2,1)S(1)}, u32[]{:S(2)}, u32[]{:S(2)}) collective-permute-start(bf16[48,3200]{1,0:T(8,128)(2,1)} %tied.34.refs_1_), channel_id=1, source_target_pairs={{0,2},{1,3},{2,0},{3,1},{4,6},{5,7},{6,4},{7,5},{8,10},{9,11},{10,... | collective-permute-start | bytes 921608 | tf_op jit(solution)/shard_map/ppermute | solution.py:98
  333.0 0.7 copy-start.12
  337.1 1.1 copy-start.3
  338.2 8.5 %collective-permute-start.9 = (bf16[24,3200]{1,0:T(8,128)(2,1)}, bf16[24,3200]{1,0:T(8,128)(2,1)S(1)}, u32[]{:S(2)}, u32[]{:S(2)}) collective-permute-start(bf16[24,3200]{1,0:T(8,128)(2,1)} %tied.36), channel_id=1, source_target_pairs={{0,4},{1,5},{2,6},{3,7},{4,0},{5,1},{6,2},{7,3},{8,12},{9,13},{10,... | collective-permute-start | bytes 460808 | tf_op jit(solution)/shard_map/ppermute | solution.py:98
  347.5 8.0 %collective-permute-start.10 = (bf16[24,3200]{1,0:T(8,128)(2,1)}, bf16[24,3200]{1,0:T(8,128)(2,1)S(1)}, u32[]{:S(2)}, u32[]{:S(2)}) collective-permute-start(bf16[24,3200]{1,0:T(8,128)(2,1)} %tied.37), channel_id=1, source_target_pairs={{0,4},{1,5},{2,6},{3,7},{4,0},{5,1},{6,2},{7,3},{8,12},{9,13},{10,... | collective-permute-start | bytes 460808 | tf_op jit(solution)/shard_map/ppermute | solution.py:98
  357.2 9.4 %collective-permute-start.11 = (bf16[48,3200]{1,0:T(8,128)(2,1)}, bf16[48,3200]{1,0:T(8,128)(2,1)S(1)}, u32[]{:S(2)}, u32[]{:S(2)}) collective-permute-start(bf16[48,3200]{1,0:T(8,128)(2,1)} %tied.38), channel_id=1, source_target_pairs={{0,2},{1,3},{2,0},{3,1},{4,6},{5,7},{6,4},{7,5},{8,10},{9,11},{10,... | collective-permute-start | bytes 921608 | tf_op jit(solution)/shard_map/ppermute | solution.py:98
  368.5 17.3 %collective-permute-start.12 = (bf16[96,3200]{1,0:T(8,128)(2,1)}, bf16[96,3200]{1,0:T(8,128)(2,1)S(1)}, u32[]{:S(2)}, u32[]{:S(2)}) collective-permute-start(bf16[96,3200]{1,0:T(8,128)(2,1)} %tied.39.refs_0_), channel_id=1, source_target_pairs={{0,1},{1,0},{2,3},{3,2},{4,5},{5,4},{6,7},{7,6},{8,9},{9,8},{10,11... | collective-permute-start | bytes 1843208 | tf_op jit(solution)/shard_map/ppermute | solution.py:98
  374.6 11.2 %copy-start.6 = (bf16[96,3200]{1,0:T(8,128)(2,1)S(1)}, bf16[96,3200]{1,0:T(8,128)(2,1)}, u32[]{:S(2)}) copy-start(bf16[96,3200]{1,0:T(8,128)(2,1)} %tied.39.refs_0_) | copy-start | bytes 1843204
  390.1 26.9 %copy-start.1 = (s32[8,1024]{1,0:T(8,128)S(1)}, s32[8,1024]{1,0:T(8,128)}, u32[]{:S(2)}) copy-start(s32[8,1024]{1,0:T(8,128)} %param.17) | copy-start | bytes 98308
Sparse Core Ops, SparseCore 0:
  10.2 35.1 all-gather.6
  46.9 70.9 all-gather.8
  165.6 70.8 reduce-scatter.1
  357.3 55.4 all-gather.10
